TPU v7x, 128 devices: a whole 4x4x4 slice. The times are simulated.
128 devices in a mesh: chan: 16 (over x, z), blk: 8 (over y, core).
Axes of the slice: x: 4, y: 4, z: 4, core: 2. Of those that a mesh axis runs over, the one named last changes fastest.
Arguments:
- pp_amps: bfloat16 [32, 3072, 3072], P('chan', 'blk'), may hold values from -6 to 6
- ph_coupling: bfloat16 [32, 3072, 3072], P('chan'), may hold values from -0.109375 to 0.109375
- pp_coupling: bfloat16 [32, 3072, 3072], P('chan', 'blk'), may hold values from -6 to 6
- sixj: float32 [2, 32, 384], replicated, may hold values from -1.5 to 1.5
- src_map: int32 [2, 32, 384], replicated, may hold values from 0 to 12287, as said below
- live_rows: int32 [32], replicated, may hold values from 1 to 3072, 49152 in all
Outputs:
- cycle_pp: bfloat16 [32, 3072, 3072], P('chan', 'blk')
- energy: float32 [], replicated
Inputs may be any that keep to these rules, and one draw needn't show every extreme that they name: For each term s, src_map[s] names every particle-particle tile exactly once. The two sources of a particle-hole tile lie in the same particle-particle channel, and in the same row block as the particle-hole tile (the rows held by one index of blk). Within one row block, the particle-hole tiles of the channels of any one chan index take their sources from every chan index equally often. `live_rows`: the largest is exactly 3072.
All inputs are finite; a program needn't handle non-finite values.
Results may differ from a plain program's by a relative error of at most 0.04.
Values may be sent and summed in bfloat16 or wider, within the bound.
No kernel may reach another device: no remote copies, remote signals or barrier semaphores. Data moves between devices by JAX's collectives and lax.ppermute only.
A program may use at most 256 MiB of HBM per device.

v0:
```python
import math

import jax
import jax.numpy as jnp
from jax import lax
from jax.sharding import PartitionSpec as P

TILE = 8


def flat_rank(source_dev, chan_count):
    matched = source_dev[..., None] == jnp.arange(chan_count, dtype=jnp.int32)
    counted = jnp.cumsum(matched.astype(jnp.int32), axis=-2) - 1
    return jnp.sum(jnp.where(matched, counted, 0), axis=-1)


def on_device(pp_amps, ph_coupling, pp_coupling, sixj, src_map, live_rows):
    chan_count = lax.axis_size("chan")
    chan_index = lax.axis_index("chan")
    blk_index = lax.axis_index("blk")
    chans_dev, rows_dev, columns = pp_amps.shape
    tiles_dev = rows_dev // TILE
    slot_count = chans_dev * tiles_dev
    bucket = slot_count // chan_count
    all_tiles = src_map.shape[2]
    slab_map = lax.dynamic_slice_in_dim(src_map, blk_index * tiles_dev, tiles_dev, 2).reshape(
        2, chan_count, slot_count
    )
    slab_coef = lax.dynamic_slice_in_dim(sixj, blk_index * tiles_dev, tiles_dev, 2).reshape(
        2, chan_count, slot_count
    )
    channel = slab_map // all_tiles
    tile_pos = slab_map % all_tiles
    source_dev = channel[0] // chans_dev
    local_slot = channel % chans_dev * tiles_dev + tile_pos % tiles_dev
    bucket_rank = flat_rank(source_dev, chan_count)
    row_base = (
        blk_index * rows_dev
        + jnp.arange(tiles_dev, dtype=jnp.int32)[:, None] * TILE
        + jnp.arange(TILE, dtype=jnp.int32)[None, :]
    )
    live_mask = (
        row_base[None, None] < live_rows.reshape(chan_count, chans_dev)[:, :, None, None]
    ).reshape(chan_count, slot_count, TILE)
    slot_ids = jnp.arange(slot_count, dtype=jnp.int32)
    wanted = (source_dev == chan_index)[:, None, :] & (
        bucket_rank[:, None, :] == jnp.arange(bucket, dtype=jnp.int32)[None, :, None]
    )
    send_slot = jnp.sum(jnp.where(wanted, slot_ids[None, None, :], 0), axis=2)
    send_index = jnp.broadcast_to(send_slot[None], (2, chan_count, bucket))
    send_loc = jnp.take_along_axis(local_slot, send_index, axis=2)
    send_coef = jnp.take_along_axis(slab_coef, send_index, axis=2)
    source_mine = jnp.take(source_dev, chan_index, axis=0)
    rank_mine = jnp.take(bucket_rank, chan_index, axis=0)
    arrival = source_mine * bucket + rank_mine
    coef_mine = jnp.take(slab_coef, chan_index, axis=1)
    mask_mine = jnp.take(live_mask, chan_index, axis=0)
    own_tiles = pp_amps.reshape(slot_count, TILE, columns)
    first_term = own_tiles[send_loc[0]]
    second_term = own_tiles[send_loc[1]]
    got_first, got_second = (
        lax.all_to_all(first_term, "chan", split_axis=0, concat_axis=0, tiled=True),
        lax.all_to_all(second_term, "chan", split_axis=0, concat_axis=0, tiled=True),
    )
    got_first = got_first.reshape(slot_count, TILE, columns)[arrival]
    got_second = got_second.reshape(slot_count, TILE, columns)[arrival]
    recoupled = coef_mine[0][:, None, None] * got_first + coef_mine[1][:, None, None] * got_second
    ph_tiles = jnp.where(mask_mine[:, :, None], recoupled, 0.0).astype(jnp.bfloat16)
    ph_rows = ph_tiles.reshape(chans_dev, rows_dev, columns)
    cycle_rows = jnp.einsum(
        "lrk,lkn->lrn", ph_rows, ph_coupling, preferred_element_type=jnp.float32
    ).astype(jnp.bfloat16)
    cycle_tiles = cycle_rows.reshape(slot_count, TILE, columns)
    order_back = jnp.sum(
        jnp.where(arrival[None, :] == slot_ids[:, None], slot_ids[None, :], 0), axis=1
    )
    back_tiles = cycle_tiles[order_back].reshape(chan_count, bucket, TILE, columns)
    returned = lax.all_to_all(back_tiles, "chan", split_axis=0, concat_axis=0, tiled=True).reshape(
        slot_count, TILE, columns
    )
    loc_flat = send_loc.reshape(2, slot_count)
    coef_flat = send_coef.reshape(2, slot_count)
    tile_source = jnp.sum(
        jnp.where(loc_flat[:, None, :] == slot_ids[None, :, None], slot_ids[None, None, :], 0),
        axis=2,
    )
    weight = jnp.take_along_axis(coef_flat, tile_source, axis=1)
    summed = (
        weight[0][:, None, None] * returned[tile_source[0]]
        + weight[1][:, None, None] * returned[tile_source[1]]
    )
    cycle_pp = summed.astype(jnp.bfloat16).reshape(chans_dev, rows_dev, columns)
    partial_energy = jnp.sum(cycle_pp.astype(jnp.float32) * pp_coupling.astype(jnp.float32))
    energy = lax.psum(partial_energy, ("chan", "blk"))
    energy = energy / (columns * math.sqrt(chan_count * chans_dev))
    return (cycle_pp, energy)


def solution(mesh):
    in_specs = (
        P("chan", "blk", None),
        P("chan", None, None),
        P("chan", "blk", None),
        P(),
        P(),
        P(),
    )
    out_specs = (P("chan", "blk", None), P())
    return jax.shard_map(
        on_device, mesh=mesh, in_specs=in_specs, out_specs=out_specs, check_vma=False
    )
```

profile of v0, /device:TPU:1, one launch (start us, length us, event | category | flops | bytes accessed | tf_op | source)
XLA Modules:
  0.0 350.2 jit_solution(11016319673521499082)
XLA Ops:
  0.7 1.0 dynamic-slice_divide_fusion
  1.6 0.9 sign_compare_fusion
  2.7 0.1 ne.69
  2.8 0.1 copy.37
  2.9 2.1 select_reduce_fusion
  5.1 0.2 select_reduce_fusion.4
  5.3 0.1 copy.39
  5.4 0.1 copy.41
  5.5 0.1 copy.40
  5.6 0.1 reshape.535
  5.7 1.9 gather_fusion.7
  7.7 0.1 reshape.538
  7.9 0.1 copy.47
  8.0 0.1 reshape.481
  8.1 5.5 %gather_fusion = bf16[96,8,3072]{2,1,0:T(8,128)(2,1)} fusion(bf16[96,8,3072]{2,1,0:T(8,128)(2,1)} %bitcast.66, s32[1024]{0:T(1024)S(1)} %pad_clamp_fusion.5), kind=kCustom, calls=%fused_computation | custom fusion | bytes 9437568 | tf_op jit(solution)/shard_map/gather | solution.py:59
  13.6 8.5 %all-to-all-start = ((bf16[16,6,8,3072]{3,2,1,0:T(8,128)(2,1)}), bf16[16,6,8,3072]{3,2,1,0:T(8,128)(2,1)}, u32[]{:S(2)}, u32[]{:S(2)}) async-start(bf16[16,6,8,3072]{3,2,1,0:T(8,128)(2,1)} %bitcast.65), calls=%async_computation | async-start | bytes 9437184 | tf_op jit(solution)/shard_map/all_to_all | solution.py:62
  22.2 0.1 copy.49
  22.3 0.1 reshape.497
  22.4 5.6 %gather_fusion.2 = bf16[96,8,3072]{2,1,0:T(8,128)(2,1)} fusion(bf16[96,8,3072]{2,1,0:T(8,128)(2,1)} %bitcast.67, s32[1024]{0:T(1024)S(1)} %pad_clamp_fusion.3), kind=kCustom, calls=%fused_computation.2 | custom fusion | bytes 9437568 | tf_op jit(solution)/shard_map/gather | solution.py:60
  27.9 65.9 %all-to-all-done = bf16[16,6,8,3072]{3,2,1,0:T(8,128)(2,1)} async-done(((bf16[16,6,8,3072]{3,2,1,0:T(8,128)(2,1)}), bf16[16,6,8,3072]{3,2,1,0:T(8,128)(2,1)}, u32[]{:S(2)}, u32[]{:S(2)}) %all-to-all-start) | async-done | bytes 4718624 | tf_op jit(solution)/shard_map/all_to_all | solution.py:62
  93.9 9.2 %all-to-all-start.1 = ((bf16[16,6,8,3072]{3,2,1,0:T(8,128)(2,1)}), bf16[16,6,8,3072]{3,2,1,0:T(8,128)(2,1)}, u32[]{:S(2)}, u32[]{:S(2)}) async-start(bf16[16,6,8,3072]{3,2,1,0:T(8,128)(2,1)} %bitcast.64), calls=%async_computation.1 | async-start | bytes 9437184 | tf_op jit(solution)/shard_map/all_to_all | solution.py:63
  103.1 0.1 gather.49
  103.2 0.1 reduce_sum.53
  103.5 0.1 mul.103
  103.6 0.1 mul.105
  103.9 0.1 mul.112
  104.2 0.1 lt.159
  104.3 0.1 compare_select_fusion
  104.4 0.1 select_n.215
  104.5 0.2 select_reduce_fusion.2
  104.8 0.1 select_reduce_fusion.3
  104.9 0.1 select_reduce_fusion.1
  105.0 5.5 %gather_fusion.1 = bf16[96,8,3072]{2,1,0:T(8,128)(2,1)} fusion(bf16[96,8,3072]{2,1,0:T(8,128)(2,1)} %bitcast.7, s32[1024]{0:T(1024)S(1)} %pad_clamp_fusion.4), kind=kCustom, calls=%fused_computation.1 | custom fusion | bytes 9437568 | tf_op jit(solution)/shard_map/gather | solution.py:65
  110.6 48.8 %all-to-all-done.1 = bf16[16,6,8,3072]{3,2,1,0:T(8,128)(2,1)} async-done(((bf16[16,6,8,3072]{3,2,1,0:T(8,128)(2,1)}), bf16[16,6,8,3072]{3,2,1,0:T(8,128)(2,1)}, u32[]{:S(2)}, u32[]{:S(2)}) %all-to-all-start.1) | async-done | bytes 4718624 | tf_op jit(solution)/shard_map/all_to_all | solution.py:63
  159.4 5.6 %gather_fusion.3 = bf16[96,8,3072]{2,1,0:T(8,128)(2,1)} fusion(bf16[96,8,3072]{2,1,0:T(8,128)(2,1)} %bitcast.12, s32[1024]{0:T(1024)S(1)} %pad_clamp_fusion.4), kind=kCustom, calls=%fused_computation.3 | custom fusion | bytes 9437568 | tf_op jit(solution)/shard_map/gather | solution.py:66
  164.9 24.0 %convolution_convert_fusion = bf16[2,384,3072]{2,1,0:T(8,128)(2,1)} fusion(bf16[2,3072,3072]{2,1,0:T(8,128)(2,1)} %param.9, bf16[2,384,3072]{2,1,0:T(8,128)(2,1)} %bitcast.71, bf16[2,384,3072]{2,1,0:T(8,128)(2,1)} %bitcast.70, f32[2,384]{1,0:T(2,128)S(1)} %mul.112, f32[2,384]{1,0:T(2,128)S(1)} %mul.105, pred[2,384]{1,0:T(4,128)(4,1)S(1)} %select_n.215), kind=kOutput, calls=%fused_computation.20 | convolution fusion | flops 14514388992 | bytes 51911424 | tf_op jit(solution)/shard_map/lrk,lkn->lrn/dot_general | solution.py:70
  188.9 5.6 %gather_fusion.4 = bf16[96,8,3072]{2,1,0:T(8,128)(2,1)} fusion(bf16[96,8,3072]{2,1,0:T(8,128)(2,1)} %bitcast.72, s32[1024]{0:T(1024)S(1)} %pad_clamp_fusion.2), kind=kCustom, calls=%fused_computation.4 | custom fusion | bytes 9437568 | tf_op jit(solution)/shard_map/gather | solution.py:77
  194.5 6.1 %all-to-all-start.2 = ((bf16[16,6,8,3072]{3,2,1,0:T(8,128)(2,1)}), bf16[16,6,8,3072]{3,2,1,0:T(8,128)(2,1)}, u32[]{:S(2)}, u32[]{:S(2)}) async-start(bf16[16,6,8,3072]{3,2,1,0:T(8,128)(2,1)} %bitcast.63), calls=%async_computation.2 | async-start | bytes 9437184 | tf_op jit(solution)/shard_map/all_to_all | solution.py:78
  200.6 1.9 gather_fusion.8
  202.7 2.0 gather_fusion.9
  204.8 0.1 mul.116
  205.0 0.1 mul.118
  205.2 0.1 mul.98
  205.4 48.7 %all-to-all-done.2 = bf16[16,6,8,3072]{3,2,1,0:T(8,128)(2,1)} async-done(((bf16[16,6,8,3072]{3,2,1,0:T(8,128)(2,1)}), bf16[16,6,8,3072]{3,2,1,0:T(8,128)(2,1)}, u32[]{:S(2)}, u32[]{:S(2)}) %all-to-all-start.2) | async-done | bytes 4718624 | tf_op jit(solution)/shard_map/all_to_all | solution.py:78
  254.1 5.5 %gather_fusion.5 = bf16[96,8,3072]{2,1,0:T(8,128)(2,1)} fusion(bf16[96,8,3072]{2,1,0:T(8,128)(2,1)} %bitcast.18, s32[1024]{0:T(1024)S(1)} %pad_clamp_fusion.1), kind=kCustom, calls=%fused_computation.5 | custom fusion | bytes 9437568 | tf_op jit(solution)/shard_map/gather | solution.py:89
  259.6 5.6 %gather_fusion.6 = bf16[96,8,3072]{2,1,0:T(8,128)(2,1)} fusion(bf16[96,8,3072]{2,1,0:T(8,128)(2,1)} %bitcast.18, s32[1024]{0:T(1024)S(1)} %pad_clamp_fusion), kind=kCustom, calls=%fused_computation.6 | custom fusion | bytes 9437568 | tf_op jit(solution)/shard_map/gather | solution.py:90
  265.2 10.2 %multiply_reduce_fusion = (f32[]{:T(128)}, bf16[2,384,3072]{2,1,0:T(8,128)(2,1)}) fusion(bf16[2,384,3072]{2,1,0:T(8,128)(2,1)} %param.10, f32[2,384]{1,0:T(2,128)S(1)} %mul.118, f32[2,384]{1,0:T(2,128)S(1)} %mul.98, bf16[2,384,3072]{2,1,0:T(8,128)(2,1)} %bitcast.69, bf16[2,384,3072]{2,1,0:T(8,128)(2,1)} %bitcast.68), kind=kLoop, calls=%fused_computation.19 | loop fusion | flops 23592960 | bytes 18880516 | tf_op jit(solution)/shard_map/reduce_sum | solution.py:93
  275.4 72.9 %psum.7 = f32[]{:T(128)} all-reduce(f32[]{:T(128)} %get-tuple-element.40), channel_id=1, replica_groups=mesh['chan'=16,'blk'=8] {'chan','blk'}, use_global_device_ids=true, to_apply=%region_6.8 | all-reduce | flops 1 | bytes 8 | tf_op jit(solution)/shard_map/psum | solution.py:94
  (54 shorter events, 1.7 us)
Async XLA Ops:
  0.6 102.6 %copy-start = (f32[2,32,384]{2,1,0:T(8,128)S(1)}, f32[2,32,384]{2,1,0:T(8,128)}, u32[]{:S(2)}) copy-start(f32[2,32,384]{2,1,0:T(8,128)} %param.11) | copy-start | bytes 294916
  13.6 80.3 %all-to-all-start = ((bf16[16,6,8,3072]{3,2,1,0:T(8,128)(2,1)}), bf16[16,6,8,3072]{3,2,1,0:T(8,128)(2,1)}, u32[]{:S(2)}, u32[]{:S(2)}) async-start(bf16[16,6,8,3072]{3,2,1,0:T(8,128)(2,1)} %bitcast.65), calls=%async_computation | async-start | bytes 9437184 | tf_op jit(solution)/shard_map/all_to_all | solution.py:62
  93.9 10.1 %copy-start.2 = (s32[32]{0:T(128)S(1)}, s32[32]{0:T(128)}, u32[]{:S(2)}) copy-start(s32[32]{0:T(128)} %param.13) | copy-start | bytes 388
  93.9 65.5 %all-to-all-start.1 = ((bf16[16,6,8,3072]{3,2,1,0:T(8,128)(2,1)}), bf16[16,6,8,3072]{3,2,1,0:T(8,128)(2,1)}, u32[]{:S(2)}, u32[]{:S(2)}) async-start(bf16[16,6,8,3072]{3,2,1,0:T(8,128)(2,1)} %bitcast.64), calls=%async_computation.1 | async-start | bytes 9437184 | tf_op jit(solution)/shard_map/all_to_all | solution.py:63
  194.5 59.6 %all-to-all-start.2 = ((bf16[16,6,8,3072]{3,2,1,0:T(8,128)(2,1)}), bf16[16,6,8,3072]{3,2,1,0:T(8,128)(2,1)}, u32[]{:S(2)}, u32[]{:S(2)}) async-start(bf16[16,6,8,3072]{3,2,1,0:T(8,128)(2,1)} %bitcast.63), calls=%async_computation.2 | async-start | bytes 9437184 | tf_op jit(solution)/shard_map/all_to_all | solution.py:78
  265.2 83.8 %copy-start.1 = (f32[2,32,384]{2,1,0:T(8,128)S(1)}, f32[2,32,384]{2,1,0:T(8,128)}, u32[]{:S(2)}) copy-start(f32[2,32,384]{2,1,0:T(8,128)} %param.11) | copy-start | bytes 294916
where the time goes:
time: 351 us; the launch traced here: 350 us
  waiting for transfers between devices  163 us (46%)
  blocking collectives  72.9 us (21%)
  local copies, waits for them, and re-layouts  48.1 us (14%)
  matrix products  24 us (7%)
  starting transfers between devices  23.8 us (7%)
  other arithmetic  15.2 us (4%)
    psum x1, blocking collectives, on_device(): energy = lax.psum(partial_energy, ('chan', 'blk'))  72.9 us
    all_to_all x1, waiting for transfers between devices, on_device(): lax.all_to_all(first_term, 'chan', split_axis=0, concat_axis=0, tiled=True)  65.9 us
    all_to_all x1, waiting for transfers between devices, on_device(): lax.all_to_all(second_term, 'chan', split_axis=0, concat_axis=0, tiled=True)  48.8 us
    all_to_all x1, waiting for transfers between devices, on_device(): lax.all_to_all(back_tiles, 'chan', split_axis=0, concat_axis=0, tiled=True)  48.7 us
    dot_general x1, matrix products, on_device(): jnp.einsum('lrk,lkn->lrn', ph_rows, ph_coupling, preferred_element_type=j...  24 us
    reduce_sum x1, other arithmetic, on_device(): jnp.sum(cycle_pp.astype(jnp.float32) * pp_coupling.astype(jnp.float32))  10.2 us
    all_to_all x1, starting transfers between devices, on_device(): lax.all_to_all(second_term, 'chan', split_axis=0, concat_axis=0, tiled=True)  9.19 us
    all_to_all x1, starting transfers between devices, on_device(): lax.all_to_all(first_term, 'chan', split_axis=0, concat_axis=0, tiled=True)  8.47 us
  transfers between devices with their start and end apart: 3, of which 3 were waited for; matrix products, arithmetic and copies ran while one was open for 5% of the time, Pallas kernels for 0%

commit v1 on v0

v1 whole, which is shorter than its diff:
```python
import math

import jax
import jax.numpy as jnp
from jax import lax
from jax.experimental import pallas as pl
from jax.experimental.pallas import tpu as pltpu
from jax.sharding import PartitionSpec as P

TILE = 8
VMEM_BYTES = 56 * 1024 * 1024


def combine_kernel(index_ref, coef_ref, tiles_ref, send_ref):
    columns = tiles_ref.shape[2]
    row = lax.broadcasted_iota(jnp.int32, (TILE, columns), 0)

    def one(slot, carry):
        first = tiles_ref[index_ref[0, slot]].astype(jnp.float32)
        second = tiles_ref[index_ref[1, slot]].astype(jnp.float32)
        value = coef_ref[0, slot] * first + coef_ref[1, slot] * second
        value = jnp.where(row < index_ref[2, slot], value, 0.0)
        send_ref[slot] = value.astype(jnp.bfloat16)
        return carry

    lax.fori_loop(0, send_ref.shape[0], one, 0, unroll=4)


def combine(index, coef, tiles, block):
    slots, _, columns = tiles.shape
    spec = pl.BlockSpec((slots, TILE, block), lambda n, *_: (0, 0, n))
    return pl.pallas_call(
        combine_kernel,
        grid_spec=pltpu.PrefetchScalarGridSpec(
            num_scalar_prefetch=2,
            grid=(columns // block,),
            in_specs=[spec],
            out_specs=spec,
        ),
        out_shape=jax.ShapeDtypeStruct(tiles.shape, jnp.bfloat16),
        compiler_params=pltpu.CompilerParams(vmem_limit_bytes=VMEM_BYTES),
        cost_estimate=pl.CostEstimate(
            flops=4 * tiles.size, bytes_accessed=4 * tiles.size, transcendentals=0
        ),
    )(index, coef, tiles)


def product_kernel(arrival_ref, x_ref, w_ref, out_ref, ordered):
    n, c = pl.program_id(0), pl.program_id(1)
    slots = x_ref.shape[0]
    half = slots // 2

    @pl.when((n == 0) & (c == 0))
    def _():
        def one(j, carry):
            ordered[j] = x_ref[arrival_ref[j]]
            return carry

        lax.fori_loop(0, slots, one, 0, unroll=4)

    rows = ordered[pl.ds(c * half, half)].reshape(half * TILE, x_ref.shape[2])
    result = jnp.dot(rows, w_ref[0], preferred_element_type=jnp.float32)
    result = result.astype(jnp.bfloat16).reshape(half, TILE, result.shape[1])
    for i in range(half):
        out_ref[arrival_ref[c * half + i]] = result[i]


def product(arrival, x, w, block):
    slots, _, columns = x.shape
    return pl.pallas_call(
        product_kernel,
        grid_spec=pltpu.PrefetchScalarGridSpec(
            num_scalar_prefetch=1,
            grid=(columns // block, 2),
            in_specs=[
                pl.BlockSpec((slots, TILE, columns), lambda n, c, *_: (0, 0, 0)),
                pl.BlockSpec((1, columns, block), lambda n, c, *_: (c, 0, n)),
            ],
            out_specs=pl.BlockSpec((slots, TILE, block), lambda n, c, *_: (0, 0, n)),
            scratch_shapes=[pltpu.VMEM((slots, TILE, columns), jnp.bfloat16)],
        ),
        out_shape=jax.ShapeDtypeStruct(x.shape, jnp.bfloat16),
        compiler_params=pltpu.CompilerParams(vmem_limit_bytes=VMEM_BYTES),
        cost_estimate=pl.CostEstimate(
            flops=2 * x.size * columns,
            bytes_accessed=4 * x.size + 2 * w.size,
            transcendentals=0,
        ),
    )(arrival, x, w)


def finish_kernel(index_ref, coef_ref, back_ref, pair_ref, out_ref, energy_ref, total):
    n = pl.program_id(0)

    @pl.when(n == 0)
    def _():
        total[...] = jnp.zeros_like(total)

    def one(g, acc):
        at0, at1 = index_ref[0, g], index_ref[1, g]
        value = coef_ref[0, at0] * back_ref[at0].astype(jnp.float32)
        value = value + coef_ref[1, at1] * back_ref[at1].astype(jnp.float32)
        out_ref[g] = value.astype(jnp.bfloat16)
        return acc + value * pair_ref[g].astype(jnp.float32)

    total[...] += lax.fori_loop(
        0, out_ref.shape[0], one, jnp.zeros(total.shape, jnp.float32), unroll=4
    )

    @pl.when(n == pl.num_programs(0) - 1)
    def _():
        sums = jnp.sum(total[...], axis=0, keepdims=True)
        energy_ref[...] = jnp.broadcast_to(jnp.sum(sums), energy_ref.shape)


def finish(index, coef, back, pair, block, copies):
    slots, _, columns = back.shape
    spec = pl.BlockSpec((slots, TILE, block), lambda n, *_: (0, 0, n))
    return pl.pallas_call(
        finish_kernel,
        grid_spec=pltpu.PrefetchScalarGridSpec(
            num_scalar_prefetch=2,
            grid=(columns // block,),
            in_specs=[spec, spec],
            out_specs=[spec, pl.BlockSpec((copies, 128), lambda n, *_: (0, 0))],
            scratch_shapes=[pltpu.VMEM((TILE, block), jnp.float32)],
        ),
        out_shape=[
            jax.ShapeDtypeStruct(back.shape, jnp.bfloat16),
            jax.ShapeDtypeStruct((copies, 128), jnp.float32),
        ],
        compiler_params=pltpu.CompilerParams(vmem_limit_bytes=VMEM_BYTES),
        cost_estimate=pl.CostEstimate(
            flops=6 * back.size, bytes_accessed=6 * back.size, transcendentals=0
        ),
    )(index, coef, back, pair)


def on_device(pp_amps, ph_coupling, pp_coupling, sixj, src_map, live_rows):
    chan_count = lax.axis_size("chan")
    blk_count = lax.axis_size("blk")
    chan_index = lax.axis_index("chan")
    blk_index = lax.axis_index("blk")
    chans_dev, rows_dev, columns = pp_amps.shape
    tiles_dev = rows_dev // TILE
    slots = chans_dev * tiles_dev
    bucket = slots // chan_count
    all_tiles = src_map.shape[2]

    def slab(array):
        part = lax.dynamic_slice_in_dim(array, blk_index * tiles_dev, tiles_dev, 2)
        return part.reshape(2, chan_count, slots)

    slab_map, slab_coef = slab(src_map), slab(sixj)
    channel = slab_map // all_tiles
    source_dev = channel[0] // chans_dev
    local_slot = channel % chans_dev * tiles_dev + slab_map % all_tiles % tiles_dev
    first_row = (blk_index * tiles_dev + jnp.arange(tiles_dev, dtype=jnp.int32)) * TILE
    live = jnp.clip(live_rows[:, None] - first_row[None, :], 0, TILE).reshape(chan_count, slots)
    ids = jnp.arange(slots, dtype=jnp.int32)

    mine = source_dev == chan_index
    before = ids[None, :] <= ids[:, None]
    rank = jnp.sum((mine[:, None, :] & before[None]).astype(jnp.int32), axis=2) - 1
    wanted = mine[:, None, :] & (
        rank[:, None, :] == jnp.arange(bucket, dtype=jnp.int32)[None, :, None]
    )

    def pick(values):
        return jnp.sum(jnp.where(wanted, values[:, None, :], 0), axis=2).reshape(slots)

    send_index = jnp.stack([pick(local_slot[0]), pick(local_slot[1]), pick(live)])
    send_coef = jnp.stack([pick(slab_coef[0]), pick(slab_coef[1])])

    source_mine = jnp.take(source_dev, chan_index, axis=0)
    earlier = (source_mine[None, :] == source_mine[:, None]) & (ids[None, :] < ids[:, None])
    arrival = source_mine * bucket + jnp.sum(earlier.astype(jnp.int32), axis=1)

    took = jnp.sum(
        jnp.where(send_index[:2, None, :] == ids[None, :, None], ids[None, None, :], 0), axis=2
    )

    send_index, send_coef, arrival, took = lax.optimization_barrier(
        (send_index, send_coef, arrival, took)
    )
    own_tiles = pp_amps.reshape(slots, TILE, columns)
    sent = combine(send_index, send_coef, own_tiles, 512)
    got = lax.all_to_all(
        sent.reshape(chan_count, bucket, TILE, columns), "chan", 0, 0, tiled=True
    ).reshape(slots, TILE, columns)
    cycle_tiles = product(arrival, got, ph_coupling, 1024)
    back = lax.all_to_all(
        cycle_tiles.reshape(chan_count, bucket, TILE, columns), "chan", 0, 0, tiled=True
    ).reshape(slots, TILE, columns)
    cycle_pp, partial = finish(
        took, send_coef, back, pp_coupling.reshape(slots, TILE, columns), 512, chan_count * blk_count
    )
    parts = lax.all_to_all(partial, ("chan", "blk"), 0, 0, tiled=True)
    energy = jnp.sum(parts[:, 0]) / (columns * math.sqrt(chan_count * chans_dev))
    return (cycle_pp.reshape(pp_amps.shape), energy)


def solution(mesh):
    in_specs = (
        P("chan", "blk", None),
        P("chan", None, None),
        P("chan", "blk", None),
        P(),
        P(),
        P(),
    )
    out_specs = (P("chan", "blk", None), P())
    return jax.shard_map(
        on_device, mesh=mesh, in_specs=in_specs, out_specs=out_specs, check_vma=False
    )
```

time: 351 us -> 195 us (0.56)
  waiting for transfers between devices: 163 us -> 0 us
  blocking collectives: 72.9 us -> 141 us
  local copies, waits for them, and re-layouts: 48.1 us -> 3.09 us
  Pallas kernels: 0 us -> 41.8 us
  matrix products: 24 us -> 0 us
  starting transfers between devices: 23.8 us -> 0 us
  other arithmetic: 15.2 us -> 5.94 us
    all_to_all x3 -> x0, waiting for transfers between devices: 163 us -> none  [the longest x1 65.9 us: on_device(): lax.all_to_all(first_term, 'chan', split_axis=0, concat_axis=0, tiled=True)]
    all_to_all x0 -> x3, blocking collectives: none -> 141 us  [the longest x1 63.4 us: on_device(): lax.all_to_all(sent.reshape(chan_count, bucket, TILE, columns), 'chan', 0...]
    psum x1 -> x0, blocking collectives: 72.9 us -> none  [on_device(): energy = lax.psum(partial_energy, ('chan', 'blk'))]
    gather x16 -> x0, local copies, waits for them, and re-layouts: 45.2 us -> none  [the longest x1 5.57 us: on_device(): second_term = own_tiles[send_loc[1]]]
    pallas_call x0 -> x3, Pallas kernels: none -> 41.8 us  [the longest x1 23.6 us: product(): pl.pallas_call(product_kernel, grid_spec=pltpu.PrefetchScalarGridSpec(num...]
    dot_general x1 -> x0, matrix products: 24 us -> none  [on_device(): jnp.einsum('lrk,lkn->lrn', ph_rows, ph_coupling, preferred_element_type=j...]
    all_to_all x3 -> x0, starting transfers between devices: 23.8 us -> none  [the longest x1 9.19 us: on_device(): lax.all_to_all(second_term, 'chan', split_axis=0, concat_axis=0, tiled=True)]
    reduce_sum x4 -> x6, other arithmetic: 10.6 us -> 2.3 us  [the longest x1 0.68 us: on_device(): jnp.sum(jnp.where(send_index[:2, None, :] == ids[None, :, None], ids[None...]
  transfers between devices with their start and end apart: 3 -> 0, of which waited for: 3 -> 0; matrix products, arithmetic and copies ran while one was open for 5% -> 0% of each run, Pallas kernels for 0% -> 0%
where the time goes in v1:
time: 195 us
  blocking collectives  141 us (72%)
  Pallas kernels  41.8 us (21%)
  other arithmetic  5.94 us (3%)
  local copies, waits for them, and re-layouts  3.09 us (2%)
  between operations  2.55 us (1%)
    all_to_all x1, blocking collectives, on_device(): lax.all_to_all(sent.reshape(chan_count, bucket, TILE, columns), 'chan', 0...  63.4 us
    all_to_all x1, blocking collectives, on_device(): lax.all_to_all(cycle_tiles.reshape(chan_count, bucket, TILE, columns), 'c...  58.3 us
    pallas_call x1, Pallas kernels, product(): pl.pallas_call(product_kernel, grid_spec=pltpu.PrefetchScalarGridSpec(num...  23.6 us
    all_to_all x1, blocking collectives, on_device(): parts = lax.all_to_all(partial, ('chan', 'blk'), 0, 0, tiled=True)  19.5 us
    pallas_call x1, Pallas kernels, finish(): pl.pallas_call(finish_kernel, grid_spec=pltpu.PrefetchScalarGridSpec(num_...  9.82 us
    pallas_call x1, Pallas kernels, combine(): pl.pallas_call(combine_kernel, grid_spec=pltpu.PrefetchScalarGridSpec(num...  8.38 us

profile of v1, /device:TPU:1, one launch (start us, length us, event | category | flops | bytes accessed | tf_op | source)
XLA Modules:
  0.0 194.6 jit_solution(6232275084705870894)
XLA Ops:
  0.7 0.9 sign_compare_fusion
  1.6 0.9 dynamic-slice_divide_fusion
  2.6 0.1 sub.48
  2.6 0.7 sub.44
  3.4 0.1 sub.45
  3.5 0.1 sub.46
  3.5 0.1 ne.61
  3.6 0.9 constant_dynamic-slice_fusion.2
  4.5 0.1 broadcast_in_dim.99
  4.6 0.1 broadcast_in_dim.96
  4.6 0.1 div.23
  4.7 0.1 rem.55
  4.9 0.2 convert_reduce_fusion.1
  5.1 0.5 multiply_add_fusion.arrival_ref
  5.6 0.3 convert_reduce_fusion
  6.0 0.1 select_reduce_fusion.2
  6.1 0.1 copy.12
  6.2 0.1 stack_reshape.18
  6.2 0.4 select_reduce_fusion.5
  6.6 0.1 copy.9
  6.7 0.1 stack_reshape.15
  6.8 0.1 copy.13
  6.9 0.1 stack_reshape.19
  7.0 0.1 copy.11
  7.1 0.1 stack_reshape.17
  7.2 0.1 copy.10
  7.2 0.1 stack_reshape.16
  7.4 0.7 select_reduce_fusion.index_ref
  8.0 0.6 pad_add_fusion.index_ref
  8.6 0.6 pad_maximum_fusion.coef_ref
  9.2 8.4 %shard_map.77 = bf16[96,8,3072]{2,1,0:T(8,128)(2,1)} custom-call(s32[3,96]{1,0:T(4,128)} %pad_add_fusion.index_ref, f32[2,96]{1,0:T(2,128)} %pad_maximum_fusion.coef_ref, bf16[96,8,3072]{2,1,0:T(8,128)(2,1)} %bitcast.29), custom_call_target="tpu_custom_call" | custom-call | flops 9437184 | bytes 9437184 | tf_op jit(solution)/shard_map/pallas_call | solution.py:32
  17.6 63.4 %all_to_all.22 = bf16[16,6,8,3072]{3,2,1,0:T(8,128)(2,1)} all-to-all(bf16[16,6,8,3072]{3,2,1,0:T(8,128)(2,1)} %bitcast.25), channel_id=1, replica_groups=mesh['chan'=16,'blk'=8] {'chan'}, dimensions={0} | all-to-all | bytes 9437184 | tf_op jit(solution)/shard_map/all_to_all | solution.py:188
  81.0 23.6 %shard_map.78 = bf16[96,8,3072]{2,1,0:T(8,128)(2,1)} custom-call(s32[96]{0:T(128)} %multiply_add_fusion.arrival_ref, bf16[96,8,3072]{2,1,0:T(8,128)(2,1)} %bitcast.27, bf16[2,3072,3072]{2,1,0:T(8,128)(2,1)} %w_ref.1), custom_call_target="tpu_custom_call" | custom-call | flops 14495514624 | bytes 47185920 | tf_op jit(solution)/shard_map/pallas_call | solution.py:70
  104.6 58.3 %all_to_all.23 = bf16[16,6,8,3072]{3,2,1,0:T(8,128)(2,1)} all-to-all(bf16[16,6,8,3072]{3,2,1,0:T(8,128)(2,1)} %bitcast.28), channel_id=1, replica_groups=mesh['chan'=16,'blk'=8] {'chan'}, dimensions={0} | all-to-all | bytes 9437184 | tf_op jit(solution)/shard_map/all_to_all | solution.py:192
  162.9 9.8 %shard_map.79 = (bf16[96,8,3072]{2,1,0:T(8,128)(2,1)}, f32[128,128]{1,0:T(8,128)}) custom-call(s32[2,96]{1,0:T(2,128)} %select_reduce_fusion.index_ref, f32[2,96]{1,0:T(2,128)} %pad_maximum_fusion.coef_ref, bf16[96,8,3072]{2,1,0:T(8,128)(2,1)} %bitcast.24, bf16[96,8,3072]{2,1,0:T(8,128)(2,1)} %bitcast.26), custom_call_target="tpu_custom_call" | custom-call | flops 14155776 | bytes 14155776 | tf_op jit(solution)/shard_map/pallas_call | solution.py:119
  172.7 19.5 %all_to_all.24 = f32[128,1,128]{2,1,0:T(1,128)S(1)} all-to-all(f32[128,1,128]{2,1,0:T(1,128)} %bitcast.31), channel_id=1, replica_groups=mesh['chan'=16,'blk'=8] {'chan','blk'}, dimensions={0} | all-to-all | bytes 131072 | tf_op jit(solution)/shard_map/all_to_all | solution.py:198
  192.2 0.6 slice_reduce_fusion
  (9 shorter events, 0.1 us)

commit v2 on v0

v2 whole, which is shorter than its diff:
```python
import functools
import math

import jax
import jax.numpy as jnp
from jax import lax
from jax.experimental import pallas as pl
from jax.experimental.pallas import tpu as pltpu
from jax.sharding import PartitionSpec as P

TILE = 8
LANES = 128
INTS = 3
COEFS = 2


def params(mib):
    return pltpu.CompilerParams(vmem_limit_bytes=mib * 1024 * 1024)


def any_spec():
    return pl.BlockSpec(memory_space=pl.ANY)


def column_copies(source, target, sems, count):
    width = source.shape[2] // count
    return [
        pltpu.make_async_copy(
            source.at[:, :, pl.ds(i * width, width)], target.at[:, :, pl.ds(i * width, width)], sems.at[i]
        )
        for i in range(count)
    ]


def floor_div(values, number):
    return jnp.floor((values.astype(jnp.float32) + 0.5) * (1.0 / number)).astype(jnp.int32)


def recouple_kernel(
    sizes, live_ref, map_hbm, sixj_hbm, tiles_ref, send_ref, ints_ref, coefs_ref, arrival_ref,
    held, made, map_ref, sixj_ref, map_buffer, sixj_buffer, ints, coefs, in_sem, out_sem, table_sem,
):
    chan_count, chans_dev, tiles_dev, all_tiles, chunks = sizes
    slots = chans_dev * tiles_dev
    bucket = slots // chan_count
    incoming = column_copies(tiles_ref, held, in_sem, chunks)
    outgoing = column_copies(made, send_ref, out_sem, chunks)
    from_hbm = [
        pltpu.make_async_copy(map_hbm, map_ref, table_sem.at[2]),
        pltpu.make_async_copy(sixj_hbm, sixj_ref, table_sem.at[3]),
    ]
    for copy in from_hbm + incoming:
        copy.start()

    me = lax.axis_index("chan")
    blk = lax.axis_index("blk")
    lane = lax.broadcasted_iota(jnp.int32, (chan_count, LANES), 1)

    def slab(ref, buffer, term):
        whole = None
        for c in range(chans_dev):
            shift = lax.rem((c - blk) * tiles_dev + all_tiles, all_tiles)
            buffer[term, c] = pltpu.roll(ref[term], shift, axis=1)[:, :LANES]
            rows = buffer[term, c, pl.ds(c, chan_count, stride=chans_dev), :]
            whole = rows if c == 0 else jnp.where(lane < c * tiles_dev, whole, rows)
        return whole

    for copy in from_hbm:
        copy.wait()
    source = None
    local = []
    for term in range(2):
        entry = slab(map_ref, map_buffer, term)
        channel = floor_div(entry, all_tiles)
        owner = floor_div(channel, chans_dev)
        tile = entry - channel * all_tiles - blk * tiles_dev
        local.append((channel - owner * chans_dev) * tiles_dev + tile)
        source = owner if source is None else source
    weight = [slab(sixj_ref, sixj_buffer, term) for term in range(2)]

    mine = (lane < slots) & (source == me)
    at = lax.broadcasted_iota(jnp.int32, (LANES, LANES), 0)
    to = lax.broadcasted_iota(jnp.int32, (LANES, LANES), 1)
    upto = (at <= to).astype(jnp.bfloat16)
    rank = jnp.dot(mine.astype(jnp.bfloat16), upto, preferred_element_type=jnp.float32)
    rank = rank.astype(jnp.int32) - 1
    int_table = jnp.zeros((chan_count, LANES), jnp.int32)
    coef_table = jnp.zeros((chan_count, LANES), jnp.float32)
    for r in range(bucket):
        chosen = mine & (rank == r)
        for f, values in enumerate((local[0], local[1], lane)):
            value = jnp.sum(jnp.where(chosen, values, 0), axis=1, keepdims=True)
            int_table = jnp.where(lane == r * INTS + f, value, int_table)
        for f, values in enumerate(weight):
            value = jnp.sum(jnp.where(chosen, values, 0.0), axis=1, keepdims=True)
            coef_table = jnp.where(lane == r * COEFS + f, value, coef_table)
    ints_ref[...] = int_table
    coefs_ref[...] = coef_table
    to_smem = [
        pltpu.make_async_copy(ints_ref, ints, table_sem.at[0]),
        pltpu.make_async_copy(coefs_ref, coefs, table_sem.at[1]),
    ]
    for copy in to_smem:
        copy.start()

    row = lax.broadcasted_iota(jnp.int32, (chan_count, LANES), 0)
    own = jnp.sum(jnp.where(row == me, source, 0), axis=0, keepdims=True)
    across = jnp.broadcast_to(own, (LANES, LANES))
    earlier = (across.T == across) & (at < to)
    arrival = own * bucket + jnp.sum(earlier.astype(jnp.int32), axis=0, keepdims=True)
    arrival_ref[...] = jnp.broadcast_to(arrival, arrival_ref.shape)

    for copy in to_smem:
        copy.wait()
    width = held.shape[2] // chunks
    tile_row = lax.broadcasted_iota(jnp.int32, (TILE, width), 0)
    for i in range(chunks):
        incoming[i].wait()
        columns = pl.ds(i * width, width)

        def to_one(d, carry):
            for r in range(bucket):
                slot = ints[d, r * INTS + 2]
                c = slot // tiles_dev
                first_row = (blk * tiles_dev + slot - c * tiles_dev) * TILE
                live = live_ref[d * chans_dev + c] - first_row
                value = coefs[d, r * COEFS] * held[ints[d, r * INTS], :, columns].astype(jnp.float32)
                value = value + coefs[d, r * COEFS + 1] * held[
                    ints[d, r * INTS + 1], :, columns
                ].astype(jnp.float32)
                value = jnp.where(tile_row < live, value, 0.0)
                made[d * bucket + r, :, columns] = value.astype(jnp.bfloat16)
            return carry

        lax.fori_loop(0, chan_count, to_one, 0)
        outgoing[i].start()
    for copy in outgoing:
        copy.wait()


def recouple(live_rows, src_map, sixj, tiles, chan_count, chans_dev, chunks=4):
    slots = tiles.shape[0]
    sizes = (chan_count, chans_dev, slots // chans_dev, src_map.shape[2], chunks)
    table = jax.ShapeDtypeStruct((chan_count, LANES), jnp.int32)
    whole = lambda shape: pl.BlockSpec(shape, lambda *_: (0,) * len(shape))
    return pl.pallas_call(
        functools.partial(recouple_kernel, sizes),
        grid_spec=pltpu.PrefetchScalarGridSpec(
            num_scalar_prefetch=1,
            grid=(1,),
            in_specs=[any_spec()] * 3,
            out_specs=[any_spec(), whole(table.shape), whole(table.shape), whole((TILE, LANES))],
            scratch_shapes=[
                pltpu.VMEM(tiles.shape, tiles.dtype),
                pltpu.VMEM(tiles.shape, tiles.dtype),
                pltpu.VMEM(src_map.shape, jnp.int32),
                pltpu.VMEM(sixj.shape, jnp.float32),
                pltpu.VMEM((2, chans_dev, src_map.shape[1], LANES), jnp.int32),
                pltpu.VMEM((2, chans_dev, src_map.shape[1], LANES), jnp.float32),
                pltpu.SMEM(table.shape, jnp.int32),
                pltpu.SMEM(table.shape, jnp.float32),
                pltpu.SemaphoreType.DMA((chunks,)),
                pltpu.SemaphoreType.DMA((chunks,)),
                pltpu.SemaphoreType.DMA((4,)),
            ],
        ),
        out_shape=[
            jax.ShapeDtypeStruct(tiles.shape, tiles.dtype),
            table,
            jax.ShapeDtypeStruct(table.shape, jnp.float32),
            jax.ShapeDtypeStruct((TILE, LANES), jnp.int32),
        ],
        compiler_params=params(60),
    )(live_rows, src_map, sixj, tiles)


def product_kernel(
    start, block, arrival_ref, x_ref, w_ref, out_ref, rows, w_held, made, x_sem, w_sem, out_sem
):
    chans_dev, _, columns = w_ref.shape
    slots = x_ref.shape[0]
    part = slots // chans_dev
    steps = out_ref.shape[2] // block
    depth = w_held.shape[0]

    def x_copy(j, c):
        return pltpu.make_async_copy(x_ref.at[arrival_ref[0, j]], rows.at[j], x_sem.at[c])

    def w_copy(n, c):
        slot = lax.rem(n * chans_dev + c, depth)
        at = pl.ds(pl.multiple_of(start + n * block, block), block)
        return pltpu.make_async_copy(w_ref.at[c, :, at], w_held.at[slot], w_sem.at[slot])

    def out_copy(n):
        at = pl.ds(pl.multiple_of(n * block, block), block)
        return pltpu.make_async_copy(made.at[:, :, at], out_ref.at[:, :, at], out_sem.at[n])

    def each(c, action):
        def one(j, carry):
            action(x_copy(j, c))
            return carry

        lax.fori_loop(c * part, (c + 1) * part, one, 0, unroll=8)

    for c in range(chans_dev):
        w_copy(0, c).start()
        each(c, lambda copy: copy.start())
    for k in range(chans_dev, min(depth, steps * chans_dev)):
        w_copy(k // chans_dev, k % chans_dev).start()

    def step(n, first):
        at = pl.ds(pl.multiple_of(n * block, block), block)
        for c in range(chans_dev):
            if first:
                each(c, lambda copy: copy.wait())
            w_copy(n, c).wait()
            left = rows[pl.ds(c * part, part)].reshape(part * TILE, columns)
            slot = lax.rem(n * chans_dev + c, depth)
            result = jnp.dot(left, w_held[slot], preferred_element_type=jnp.float32)
            result = result.astype(jnp.bfloat16).reshape(part, TILE, block)
            for i in range(part):
                made[arrival_ref[0, c * part + i], :, at] = result[i]

            @pl.when(n + depth // chans_dev < steps)
            def _():
                w_copy(n + depth // chans_dev, c).start()

        out_copy(n).start()

    step(jnp.int32(0), True)

    def body(n, carry):
        step(n, False)
        return carry

    lax.fori_loop(1, steps, body, 0)
    for n in range(steps):
        out_copy(n).wait()


def product(arrival, x, w, start, width, block=256, depth=24):
    chans_dev, columns, _ = w.shape
    depth = min(depth, chans_dev * (width // block))
    made = jax.ShapeDtypeStruct(x.shape[:2] + (width,), x.dtype)
    return pl.pallas_call(
        functools.partial(product_kernel, start, block),
        grid_spec=pltpu.PrefetchScalarGridSpec(
            num_scalar_prefetch=1,
            grid=(1,),
            in_specs=[any_spec(), any_spec()],
            out_specs=any_spec(),
            scratch_shapes=[
                pltpu.VMEM(x.shape, x.dtype),
                pltpu.VMEM((depth, columns, block), w.dtype),
                pltpu.VMEM(made.shape, x.dtype),
                pltpu.SemaphoreType.DMA((chans_dev,)),
                pltpu.SemaphoreType.DMA((depth,)),
                pltpu.SemaphoreType.DMA((width // block,)),
            ],
        ),
        out_shape=made,
        compiler_params=params(60),
    )(arrival, x, w)


def finish_kernel(
    bucket, chunks, ints_ref, coefs_ref, back_ref, pair_ref, out_ref, energy_ref,
    back, pair, made, slot_of, weight_of, back_sem, pair_sem, out_sem,
):
    slots = back.shape[0]
    back_in = column_copies(back_ref, back, back_sem, chunks)
    pair_in = column_copies(pair_ref, pair, pair_sem, chunks)
    outgoing = column_copies(made, out_ref, out_sem, chunks)
    for i in range(chunks):
        back_in[i].start()
        pair_in[i].start()

    def invert(d, carry):
        for r in range(bucket):
            for term in range(2):
                g = ints_ref[d, r * INTS + term]
                slot_of[term, g] = d * bucket + r
                weight_of[term, g] = coefs_ref[d, r * COEFS + term]
        return carry

    lax.fori_loop(0, slots // bucket, invert, 0)
    width = back.shape[2] // chunks
    total = jnp.zeros((TILE, width), jnp.float32)
    for i in range(chunks):
        back_in[i].wait()
        pair_in[i].wait()
        columns = pl.ds(i * width, width)

        def one(g, total):
            value = weight_of[0, g] * back[slot_of[0, g], :, columns].astype(jnp.float32)
            value = value + weight_of[1, g] * back[slot_of[1, g], :, columns].astype(jnp.float32)
            made[g, :, columns] = value.astype(jnp.bfloat16)
            return total + value * pair[g, :, columns].astype(jnp.float32)

        total = lax.fori_loop(0, slots, one, total, unroll=8)
        outgoing[i].start()
    total = jnp.sum(jnp.sum(total, axis=0, keepdims=True), axis=1, keepdims=True)
    energy_ref[...] = jnp.broadcast_to(total, energy_ref.shape)
    for copy in outgoing:
        copy.wait()


def finish(ints, coefs, back, pair, copies, chunks=4):
    slots = back.shape[0]
    bucket = slots // ints.shape[0]
    return pl.pallas_call(
        functools.partial(finish_kernel, bucket, chunks),
        grid_spec=pltpu.PrefetchScalarGridSpec(
            num_scalar_prefetch=2,
            grid=(1,),
            in_specs=[any_spec(), any_spec()],
            out_specs=[any_spec(), pl.BlockSpec((copies, LANES), lambda *_: (0, 0))],
            scratch_shapes=[
                pltpu.VMEM(back.shape, back.dtype),
                pltpu.VMEM(back.shape, back.dtype),
                pltpu.VMEM(back.shape, back.dtype),
                pltpu.SMEM((2, slots), jnp.int32),
                pltpu.SMEM((2, slots), jnp.float32),
                pltpu.SemaphoreType.DMA((chunks,)),
                pltpu.SemaphoreType.DMA((chunks,)),
                pltpu.SemaphoreType.DMA((chunks,)),
            ],
        ),
        out_shape=[
            jax.ShapeDtypeStruct(back.shape, back.dtype),
            jax.ShapeDtypeStruct((copies, LANES), jnp.float32),
        ],
        compiler_params=params(56),
    )(ints, coefs, back, pair)


def exchange(tiles, chan_count):
    parts = tiles.reshape((chan_count, -1) + tiles.shape[1:])
    return lax.all_to_all(parts, "chan", 0, 0, tiled=True).reshape(tiles.shape)


def on_device(pp_amps, ph_coupling, pp_coupling, sixj, src_map, live_rows):
    chan_count = lax.axis_size("chan")
    blk_count = lax.axis_size("blk")
    chans_dev, rows_dev, columns = pp_amps.shape
    slots = chans_dev * rows_dev // TILE
    own_tiles = pp_amps.reshape(slots, TILE, columns)
    pair_tiles = pp_coupling.reshape(slots, TILE, columns)
    sent, ints, coefs, arrival = recouple(
        live_rows, src_map, sixj, own_tiles, chan_count, chans_dev
    )
    got = exchange(sent, chan_count)
    back = exchange(product(arrival, got, ph_coupling, 0, columns, 512, 12), chan_count)
    cycle_pp, partial = finish(ints, coefs, back, pair_tiles, chan_count * blk_count)
    parts = lax.all_to_all(partial, ("chan", "blk"), 0, 0, tiled=True)
    energy = jnp.sum(parts[:, 0]) / (columns * math.sqrt(chan_count * chans_dev))
    return (cycle_pp.reshape(pp_amps.shape), energy)


def solution(mesh):
    in_specs = (
        P("chan", "blk", None),
        P("chan", None, None),
        P("chan", "blk", None),
        P(),
        P(),
        P(),
    )
    out_specs = (P("chan", "blk", None), P())
    return jax.shard_map(
        on_device, mesh=mesh, in_specs=in_specs, out_specs=out_specs, check_vma=False
    )
```

time: 351 us -> 184 us (0.52)
  waiting for transfers between devices: 163 us -> 0 us
  blocking collectives: 72.9 us -> 141 us
  local copies, waits for them, and re-layouts: 48.1 us -> 0 us
  Pallas kernels: 0 us -> 38.9 us
  matrix products: 24 us -> 0 us
  starting transfers between devices: 23.8 us -> 0 us
  other arithmetic: 15.2 us -> 0.62 us
    all_to_all x3 -> x0, waiting for transfers between devices: 163 us -> none  [the longest x1 65.9 us: on_device(): lax.all_to_all(first_term, 'chan', split_axis=0, concat_axis=0, tiled=True)]
    all_to_all x0 -> x3, blocking collectives: none -> 141 us  [the longest x2 122 us: exchange(): return lax.all_to_all(parts, 'chan', 0, 0, tiled=True).reshape(tiles.shape)]
    psum x1 -> x0, blocking collectives: 72.9 us -> none  [on_device(): energy = lax.psum(partial_energy, ('chan', 'blk'))]
    gather x16 -> x0, local copies, waits for them, and re-layouts: 45.2 us -> none  [the longest x1 5.57 us: on_device(): second_term = own_tiles[send_loc[1]]]
    pallas_call x0 -> x3, Pallas kernels: none -> 38.9 us  [the longest x1 21.2 us: product(): pl.pallas_call(functools.partial(product_kernel, start, block), grid_spec...]
    dot_general x1 -> x0, matrix products: 24 us -> none  [on_device(): jnp.einsum('lrk,lkn->lrn', ph_rows, ph_coupling, preferred_element_type=j...]
    all_to_all x3 -> x0, starting transfers between devices: 23.8 us -> none  [the longest x1 9.19 us: on_device(): lax.all_to_all(second_term, 'chan', split_axis=0, concat_axis=0, tiled=True)]
    reduce_sum x4 -> x1, other arithmetic: 10.6 us -> 0.62 us  [on_device(): jnp.sum(parts[:, 0]) / (columns * math.sqrt(chan_count * chans_dev))]
  transfers between devices with their start and end apart: 3 -> 0, of which waited for: 3 -> 0; matrix products, arithmetic and copies ran while one was open for 5% -> 0% of each run, Pallas kernels for 0% -> 0%
where the time goes in v2:
time: 184 us; the launch traced here: 183 us
  blocking collectives  141 us (77%)
  Pallas kernels  38.9 us (21%)
  between operations  2.43 us (1%)
    all_to_all x2, blocking collectives, exchange(): return lax.all_to_all(parts, 'chan', 0, 0, tiled=True).reshape(tiles.shape)  122 us
    pallas_call x1, Pallas kernels, product(): pl.pallas_call(functools.partial(product_kernel, start, block), grid_spec...  21.2 us
    all_to_all x1, blocking collectives, on_device(): parts = lax.all_to_all(partial, ('chan', 'blk'), 0, 0, tiled=True)  19.5 us
    pallas_call x1, Pallas kernels, recouple(): pl.pallas_call(functools.partial(recouple_kernel, sizes), grid_spec=pltpu...  9.91 us
    pallas_call x1, Pallas kernels, finish(): pl.pallas_call(functools.partial(finish_kernel, bucket, chunks), grid_spe...  7.78 us

profile of v2, /device:TPU:1, one launch (start us, length us, event | category | flops | bytes accessed | tf_op | source)
XLA Modules:
  0.0 183.1 jit_solution(17599900147805205702)
XLA Ops:
  0.6 9.9 %shard_map.77 = (bf16[96,8,3072]{2,1,0:T(8,128)(2,1)}, s32[16,128]{1,0:T(8,128)}, f32[16,128]{1,0:T(8,128)}, s32[8,128]{1,0:T(8,128)}) custom-call(s32[32]{0:T(128)} %live_ref.1, s32[2,32,384]{2,1,0:T(8,128)} %map_hbm.1, f32[2,32,384]{2,1,0:T(8,128)} %sixj_hbm.1, bf16[96,8,3072]{2,1,0:T(8,128)(2,1)} %bitcast.14), custom_call_target="tpu_custom_call" | custom-call | tf_op jit(solution)/shard_map/pallas_call | solution.py:146
  10.5 63.4 %all_to_all.22 = bf16[16,6,8,3072]{3,2,1,0:T(8,128)(2,1)} all-to-all(bf16[16,6,8,3072]{3,2,1,0:T(8,128)(2,1)} %bitcast.16), channel_id=1, replica_groups=mesh['chan'=16,'blk'=8] {'chan'}, dimensions={0} | all-to-all | bytes 9437184 | tf_op jit(solution)/shard_map/all_to_all | solution.py:339
  73.9 21.2 %shard_map.78 = bf16[96,8,3072]{2,1,0:T(8,128)(2,1)} custom-call(s32[8,128]{1,0:T(8,128)} %get-tuple-element.10.arrival_ref, bf16[96,8,3072]{2,1,0:T(8,128)(2,1)} %bitcast.11, bf16[2,3072,3072]{2,1,0:T(8,128)(2,1)} %w_ref.1), custom_call_target="tpu_custom_call" | custom-call | tf_op jit(solution)/shard_map/pallas_call | solution.py:245
  95.1 58.3 %all_to_all.23 = bf16[16,6,8,3072]{3,2,1,0:T(8,128)(2,1)} all-to-all(bf16[16,6,8,3072]{3,2,1,0:T(8,128)(2,1)} %bitcast.12), channel_id=1, replica_groups=mesh['chan'=16,'blk'=8] {'chan'}, dimensions={0} | all-to-all | bytes 9437184 | tf_op jit(solution)/shard_map/all_to_all | solution.py:339
  153.5 7.8 %shard_map.79 = (bf16[96,8,3072]{2,1,0:T(8,128)(2,1)}, f32[128,128]{1,0:T(8,128)}) custom-call(s32[16,128]{1,0:T(8,128)} %get-tuple-element.8.ints_ref, f32[16,128]{1,0:T(8,128)} %get-tuple-element.9.coefs_ref, bf16[96,8,3072]{2,1,0:T(8,128)(2,1)} %bitcast.13, bf16[96,8,3072]{2,1,0:T(8,128)(2,1)} %bitcast.15), custom_call_target="tpu_custom_call" | custom-call | tf_op jit(solution)/shard_map/pallas_call | solution.py:311
  161.3 19.5 %all_to_all.24 = f32[128,1,128]{2,1,0:T(1,128)S(1)} all-to-all(f32[128,1,128]{2,1,0:T(1,128)} %bitcast.18), channel_id=1, replica_groups=mesh['chan'=16,'blk'=8] {'chan','blk'}, dimensions={0} | all-to-all | bytes 131072 | tf_op jit(solution)/shard_map/all_to_all | solution.py:355
  180.7 0.6 slice_reduce_fusion

commit v3 on v2

--- a/solution.py
+++ b/solution.py
@@ -10,16 +10,17 @@
 
 TILE = 8
 LANES = 128
-INTS = 3
-COEFS = 2
+BITS = 8
+LOW = (1 << BITS) - 1
+WIDTHS = (1024, 2048)
 
 
 def params(mib):
     return pltpu.CompilerParams(vmem_limit_bytes=mib * 1024 * 1024)
 
 
-def any_spec():
-    return pl.BlockSpec(memory_space=pl.ANY)
+def hbm_spec():
+    return pl.BlockSpec(memory_space=pltpu.HBM)
 
 
 def column_copies(source, target, sems, count):
@@ -37,8 +38,8 @@
 
 
 def recouple_kernel(
-    sizes, live_ref, map_hbm, sixj_hbm, tiles_ref, send_ref, ints_ref, coefs_ref, arrival_ref,
-    held, made, map_ref, sixj_ref, map_buffer, sixj_buffer, ints, coefs, in_sem, out_sem, table_sem,
+    sizes, live_hbm, map_hbm, sixj_hbm, tiles_ref, send_ref, ints_ref, coefs_ref, arrival_ref,
+    held, made, live_ref, map_ref, sixj_ref, map_buffer, sixj_buffer, ints, coefs, in_sem, out_sem, table_sem,
 ):
     chan_count, chans_dev, tiles_dev, all_tiles, chunks = sizes
     slots = chans_dev * tiles_dev
@@ -48,8 +49,9 @@
     from_hbm = [
         pltpu.make_async_copy(map_hbm, map_ref, table_sem.at[2]),
         pltpu.make_async_copy(sixj_hbm, sixj_ref, table_sem.at[3]),
+        pltpu.make_async_copy(live_hbm, live_ref, table_sem.at[4]),
     ]
-    for copy in from_hbm + incoming:
+    for copy in from_hbm + incoming[:1]:
         copy.start()
 
     me = lax.axis_index("chan")
@@ -84,23 +86,23 @@
     upto = (at <= to).astype(jnp.bfloat16)
     rank = jnp.dot(mine.astype(jnp.bfloat16), upto, preferred_element_type=jnp.float32)
     rank = rank.astype(jnp.int32) - 1
+    packed = local[0] + (local[1] << BITS) + (lane << 2 * BITS)
     int_table = jnp.zeros((chan_count, LANES), jnp.int32)
     coef_table = jnp.zeros((chan_count, LANES), jnp.float32)
     for r in range(bucket):
         chosen = mine & (rank == r)
-        for f, values in enumerate((local[0], local[1], lane)):
-            value = jnp.sum(jnp.where(chosen, values, 0), axis=1, keepdims=True)
-            int_table = jnp.where(lane == r * INTS + f, value, int_table)
-        for f, values in enumerate(weight):
+        value = jnp.sum(jnp.where(chosen, packed, 0), axis=1, keepdims=True)
+        int_table = jnp.where(lane == r, value, int_table)
+        for term, values in enumerate(weight):
             value = jnp.sum(jnp.where(chosen, values, 0.0), axis=1, keepdims=True)
-            coef_table = jnp.where(lane == r * COEFS + f, value, coef_table)
+            coef_table = jnp.where(lane == 2 * r + term, value, coef_table)
     ints_ref[...] = int_table
     coefs_ref[...] = coef_table
     to_smem = [
         pltpu.make_async_copy(ints_ref, ints, table_sem.at[0]),
         pltpu.make_async_copy(coefs_ref, coefs, table_sem.at[1]),
     ]
-    for copy in to_smem:
+    for copy in to_smem + incoming[1:]:
         copy.start()
 
     row = lax.broadcasted_iota(jnp.int32, (chan_count, LANES), 0)
@@ -120,14 +122,14 @@
 
         def to_one(d, carry):
             for r in range(bucket):
-                slot = ints[d, r * INTS + 2]
-                c = slot // tiles_dev
+                entry = ints[d, r]
+                slot = entry >> 2 * BITS
+                c = sum((slot >= k * tiles_dev).astype(jnp.int32) for k in range(1, chans_dev))
                 first_row = (blk * tiles_dev + slot - c * tiles_dev) * TILE
                 live = live_ref[d * chans_dev + c] - first_row
-                value = coefs[d, r * COEFS] * held[ints[d, r * INTS], :, columns].astype(jnp.float32)
-                value = value + coefs[d, r * COEFS + 1] * held[
-                    ints[d, r * INTS + 1], :, columns
-                ].astype(jnp.float32)
+                first = held[entry & LOW, :, columns].astype(jnp.float32)
+                second = held[(entry >> BITS) & LOW, :, columns].astype(jnp.float32)
+                value = coefs[d, 2 * r] * first + coefs[d, 2 * r + 1] * second
                 value = jnp.where(tile_row < live, value, 0.0)
                 made[d * bucket + r, :, columns] = value.astype(jnp.bfloat16)
             return carry
@@ -138,21 +140,20 @@
         copy.wait()
 
 
-def recouple(live_rows, src_map, sixj, tiles, chan_count, chans_dev, chunks=4):
+def recouple(live_rows, src_map, sixj, tiles, chan_count, chans_dev, chunks=3):
     slots = tiles.shape[0]
     sizes = (chan_count, chans_dev, slots // chans_dev, src_map.shape[2], chunks)
     table = jax.ShapeDtypeStruct((chan_count, LANES), jnp.int32)
-    whole = lambda shape: pl.BlockSpec(shape, lambda *_: (0,) * len(shape))
     return pl.pallas_call(
         functools.partial(recouple_kernel, sizes),
         grid_spec=pltpu.PrefetchScalarGridSpec(
-            num_scalar_prefetch=1,
-            grid=(1,),
-            in_specs=[any_spec()] * 3,
-            out_specs=[any_spec(), whole(table.shape), whole(table.shape), whole((TILE, LANES))],
+            num_scalar_prefetch=0,
+            in_specs=[hbm_spec()] * 4,
+            out_specs=[hbm_spec()] + [pl.BlockSpec(memory_space=pltpu.VMEM)] * 3,
             scratch_shapes=[
                 pltpu.VMEM(tiles.shape, tiles.dtype),
                 pltpu.VMEM(tiles.shape, tiles.dtype),
+                pltpu.SMEM(live_rows.shape, jnp.int32),
                 pltpu.VMEM(src_map.shape, jnp.int32),
                 pltpu.VMEM(sixj.shape, jnp.float32),
                 pltpu.VMEM((2, chans_dev, src_map.shape[1], LANES), jnp.int32),
@@ -161,7 +162,7 @@
                 pltpu.SMEM(table.shape, jnp.float32),
                 pltpu.SemaphoreType.DMA((chunks,)),
                 pltpu.SemaphoreType.DMA((chunks,)),
-                pltpu.SemaphoreType.DMA((4,)),
+                pltpu.SemaphoreType.DMA((5,)),
             ],
         ),
         out_shape=[
@@ -170,12 +171,13 @@
             jax.ShapeDtypeStruct(table.shape, jnp.float32),
             jax.ShapeDtypeStruct((TILE, LANES), jnp.int32),
         ],
-        compiler_params=params(60),
+        compiler_params=params(63),
     )(live_rows, src_map, sixj, tiles)
 
 
 def product_kernel(
-    start, block, arrival_ref, x_ref, w_ref, out_ref, rows, w_held, made, x_sem, w_sem, out_sem
+    start, block, arrival_hbm, x_ref, w_ref, out_ref,
+    arrival_ref, rows, w_held, made, x_sem, w_sem, out_sem, table_sem,
 ):
     chans_dev, _, columns = w_ref.shape
     slots = x_ref.shape[0]
@@ -202,8 +204,13 @@
 
         lax.fori_loop(c * part, (c + 1) * part, one, 0, unroll=8)
 
+    table = pltpu.make_async_copy(arrival_hbm, arrival_ref, table_sem)
+    table.start()
+    w_copy(0, 0).start()
+    table.wait()
     for c in range(chans_dev):
-        w_copy(0, c).start()
+        if c:
+            w_copy(0, c).start()
         each(c, lambda copy: copy.start())
     for k in range(chans_dev, min(depth, steps * chans_dev)):
         w_copy(k // chans_dev, k % chans_dev).start()
@@ -238,100 +245,132 @@
         out_copy(n).wait()
 
 
-def product(arrival, x, w, start, width, block=256, depth=24):
+def product(arrival, x, w, start, width, block=512, depth=12):
     chans_dev, columns, _ = w.shape
     depth = min(depth, chans_dev * (width // block))
     made = jax.ShapeDtypeStruct(x.shape[:2] + (width,), x.dtype)
     return pl.pallas_call(
         functools.partial(product_kernel, start, block),
         grid_spec=pltpu.PrefetchScalarGridSpec(
-            num_scalar_prefetch=1,
-            grid=(1,),
-            in_specs=[any_spec(), any_spec()],
-            out_specs=any_spec(),
+            num_scalar_prefetch=0,
+            in_specs=[hbm_spec()] * 3,
+            out_specs=hbm_spec(),
             scratch_shapes=[
+                pltpu.SMEM(arrival.shape, jnp.int32),
                 pltpu.VMEM(x.shape, x.dtype),
                 pltpu.VMEM((depth, columns, block), w.dtype),
                 pltpu.VMEM(made.shape, x.dtype),
                 pltpu.SemaphoreType.DMA((chans_dev,)),
                 pltpu.SemaphoreType.DMA((depth,)),
                 pltpu.SemaphoreType.DMA((width // block,)),
+                pltpu.SemaphoreType.DMA,
             ],
         ),
         out_shape=made,
-        compiler_params=params(60),
+        compiler_params=params(63),
+        cost_estimate=pl.CostEstimate(
+            flops=2 * x.size * width,
+            bytes_accessed=2 * (x.size + made.size + chans_dev * columns * width),
+            transcendentals=0,
+        ),
     )(arrival, x, w)
 
 
-def finish_kernel(
-    bucket, chunks, ints_ref, coefs_ref, back_ref, pair_ref, out_ref, energy_ref,
-    back, pair, made, slot_of, weight_of, back_sem, pair_sem, out_sem,
-):
-    slots = back.shape[0]
-    back_in = column_copies(back_ref, back, back_sem, chunks)
-    pair_in = column_copies(pair_ref, pair, pair_sem, chunks)
-    outgoing = column_copies(made, out_ref, out_sem, chunks)
-    for i in range(chunks):
-        back_in[i].start()
-        pair_in[i].start()
+def finish_kernel(start, chunks, adds, writes, ints_hbm, coefs_hbm, back_ref, pair_ref, *refs):
+    refs = list(refs)
+    if start and writes:
+        refs.pop(0)
+    before_ref = refs.pop(0) if start and adds else None
+    out_ref = refs.pop(0) if writes else None
+    energy_ref = refs.pop(0) if adds else None
+    ints_ref, coefs_ref, back, pair, made, slot_of, weight_of, back_sem, pair_sem, out_sem, table_sem = refs
+    slots, _, columns = back.shape
+    bucket = slots // ints_ref.shape[0]
+    here = pl.ds(start, columns)
+    incoming = [column_copies(back_ref, back, back_sem, chunks)]
+    if adds:
+        incoming.append(column_copies(pair_ref.at[:, :, here], pair, pair_sem, chunks))
+    outgoing = column_copies(made, out_ref.at[:, :, here], out_sem, chunks) if writes else []
+    tables = [
+        pltpu.make_async_copy(ints_hbm, ints_ref, table_sem.at[0]),
+        pltpu.make_async_copy(coefs_hbm, coefs_ref, table_sem.at[1]),
+    ]
+    for copies in [tables] + list(zip(*incoming)):
+        for copy in copies:
+            copy.start()
+    for copy in tables:
+        copy.wait()
 
     def invert(d, carry):
         for r in range(bucket):
+            entry = ints_ref[d, r]
             for term in range(2):
-                g = ints_ref[d, r * INTS + term]
+                g = (entry >> (term * BITS)) & LOW
                 slot_of[term, g] = d * bucket + r
-                weight_of[term, g] = coefs_ref[d, r * COEFS + term]
+                weight_of[term, g] = coefs_ref[d, 2 * r + term]
         return carry
 
     lax.fori_loop(0, slots // bucket, invert, 0)
-    width = back.shape[2] // chunks
+    width = columns // chunks
     total = jnp.zeros((TILE, width), jnp.float32)
     for i in range(chunks):
-        back_in[i].wait()
-        pair_in[i].wait()
-        columns = pl.ds(i * width, width)
+        for copies in incoming:
+            copies[i].wait()
+        at = pl.ds(i * width, width)
 
         def one(g, total):
-            value = weight_of[0, g] * back[slot_of[0, g], :, columns].astype(jnp.float32)
-            value = value + weight_of[1, g] * back[slot_of[1, g], :, columns].astype(jnp.float32)
-            made[g, :, columns] = value.astype(jnp.bfloat16)
-            return total + value * pair[g, :, columns].astype(jnp.float32)
+            value = weight_of[0, g] * back[slot_of[0, g], :, at].astype(jnp.float32)
+            value = value + weight_of[1, g] * back[slot_of[1, g], :, at].astype(jnp.float32)
+            value = value.astype(jnp.bfloat16)
+            if writes:
+                made[g, :, at] = value
+            if adds:
+                total = total + value.astype(jnp.float32) * pair[g, :, at].astype(jnp.float32)
+            return total
 
         total = lax.fori_loop(0, slots, one, total, unroll=8)
-        outgoing[i].start()
-    total = jnp.sum(jnp.sum(total, axis=0, keepdims=True), axis=1, keepdims=True)
-    energy_ref[...] = jnp.broadcast_to(total, energy_ref.shape)
+        if writes:
+            outgoing[i].start()
+    if adds:
+        total = jnp.sum(jnp.sum(total, axis=0, keepdims=True), axis=1, keepdims=True)
+        total = jnp.broadcast_to(total, energy_ref.shape)
+        energy_ref[...] = total + before_ref[...] if start else total
     for copy in outgoing:
         copy.wait()
 
 
-def finish(ints, coefs, back, pair, copies, chunks=4):
-    slots = back.shape[0]
-    bucket = slots // ints.shape[0]
+def finish(ints, coefs, back, pair, start, written, added, copies, chunks, adds=True, writes=True):
+    energy = pl.BlockSpec(memory_space=pltpu.VMEM)
+    again, more = bool(start and writes), bool(start and adds)
+    outs = [(hbm_spec(), jax.ShapeDtypeStruct(pair.shape, pair.dtype))] * writes
+    outs = outs + [(energy, jax.ShapeDtypeStruct((copies, LANES), jnp.float32))] * adds
     return pl.pallas_call(
-        functools.partial(finish_kernel, bucket, chunks),
+        functools.partial(finish_kernel, start, chunks, adds, writes),
         grid_spec=pltpu.PrefetchScalarGridSpec(
-            num_scalar_prefetch=2,
-            grid=(1,),
-            in_specs=[any_spec(), any_spec()],
-            out_specs=[any_spec(), pl.BlockSpec((copies, LANES), lambda *_: (0, 0))],
+            num_scalar_prefetch=0,
+            in_specs=[hbm_spec()] * (4 + again) + [energy] * more,
+            out_specs=[spec for spec, _ in outs],
             scratch_shapes=[
+                pltpu.SMEM(ints.shape, jnp.int32),
+                pltpu.SMEM(coefs.shape, jnp.float32),
                 pltpu.VMEM(back.shape, back.dtype),
                 pltpu.VMEM(back.shape, back.dtype),
                 pltpu.VMEM(back.shape, back.dtype),
-                pltpu.SMEM((2, slots), jnp.int32),
-                pltpu.SMEM((2, slots), jnp.float32),
+                pltpu.SMEM((2, back.shape[0]), jnp.int32),
+                pltpu.SMEM((2, back.shape[0]), jnp.float32),
                 pltpu.SemaphoreType.DMA((chunks,)),
                 pltpu.SemaphoreType.DMA((chunks,)),
                 pltpu.SemaphoreType.DMA((chunks,)),
+                pltpu.SemaphoreType.DMA((2,)),
             ],
         ),
-        out_shape=[
-            jax.ShapeDtypeStruct(back.shape, back.dtype),
-            jax.ShapeDtypeStruct((copies, LANES), jnp.float32),
-        ],
-        compiler_params=params(56),
-    )(ints, coefs, back, pair)
+        out_shape=[shape for _, shape in outs],
+        input_output_aliases={4: 0} if again else {},
+        compiler_params=params(63),
+        cost_estimate=pl.CostEstimate(
+            flops=6 * back.size, bytes_accessed=6 * back.size, transcendentals=0
+        ),
+    )(ints, coefs, back, pair, *[written] * again, *[added] * more)
 
 
 def exchange(tiles, chan_count):
@@ -350,8 +389,21 @@
         live_rows, src_map, sixj, own_tiles, chan_count, chans_dev
     )
     got = exchange(sent, chan_count)
-    back = exchange(product(arrival, got, ph_coupling, 0, columns, 512, 12), chan_count)
-    cycle_pp, partial = finish(ints, coefs, back, pair_tiles, chan_count * blk_count)
+    cycle_pp = partial = None
+    start = 0
+    for width in WIDTHS:
+        made = product(arrival, got, ph_coupling, start, width)
+        back = exchange(made, chan_count)
+        chunks = max(1, 4 * width // columns)
+        call = functools.partial(
+            finish, ints, coefs, back, pair_tiles, start, cycle_pp, partial, chan_count * blk_count, chunks
+        )
+        start += width
+        if start < columns:
+            cycle_pp, partial = call()
+        else:
+            (partial,) = call(writes=False)
+            (cycle_pp,) = call(adds=False)
     parts = lax.all_to_all(partial, ("chan", "blk"), 0, 0, tiled=True)
     energy = jnp.sum(parts[:, 0]) / (columns * math.sqrt(chan_count * chans_dev))
     return (cycle_pp.reshape(pp_amps.shape), energy)

time: 184 us -> 178 us (0.967)
  blocking collectives: 141 us -> 63.4 us
  waiting for transfers between devices: 0 us -> 41 us
  starting transfers between devices: 0 us -> 24.4 us
  Pallas kernels: 38.9 us -> 45.7 us
    all_to_all x2 -> x1, blocking collectives: 122 us -> 63.4 us  [exchange(): return lax.all_to_all(parts, 'chan', 0, 0, tiled=True).reshape(tiles.shape)]
    all_to_all x0 -> x3, waiting for transfers between devices: none -> 41 us  [the longest x2 35.8 us: exchange(): return lax.all_to_all(parts, 'chan', 0, 0, tiled=True).reshape(tiles.shape)]
    all_to_all x0 -> x3, starting transfers between devices: none -> 24.4 us  [the longest x1 14.9 us: on_device(): parts = lax.all_to_all(partial, ('chan', 'blk'), 0, 0, tiled=True)]
    all_to_all x1 -> x0, blocking collectives: 19.5 us -> none  [on_device(): parts = lax.all_to_all(partial, ('chan', 'blk'), 0, 0, tiled=True)]
    pallas_call x1 -> x3, Pallas kernels: 7.78 us -> 14.8 us  [finish(): pl.pallas_call(functools.partial(finish_kernel, start, chunks, adds, writ...]
    pallas_call x1, Pallas kernels: 9.91 us -> 6.56 us  [recouple(): pl.pallas_call(functools.partial(recouple_kernel, sizes), grid_spec=pltpu...]
    pallas_call x1 -> x2, Pallas kernels: 21.2 us -> 24.3 us  [product(): pl.pallas_call(functools.partial(product_kernel, start, block), grid_spec...]
  transfers between devices with their start and end apart: 0 -> 3, of which waited for: 0 -> 3; matrix products, arithmetic and copies ran while one was open for 0% -> 0% of each run, Pallas kernels for 0% -> 14%
where the time goes in v3:
time: 178 us
  blocking collectives  63.4 us (36%)
  Pallas kernels  45.7 us (26%)
  waiting for transfers between devices  41 us (23%)
  starting transfers between devices  24.4 us (14%)
  between operations  2.48 us (1%)
    all_to_all x1, blocking collectives, exchange(): return lax.all_to_all(parts, 'chan', 0, 0, tiled=True).reshape(tiles.shape)  63.4 us
    all_to_all x2, waiting for transfers between devices, exchange(): return lax.all_to_all(parts, 'chan', 0, 0, tiled=True).reshape(tiles.shape)  35.8 us
    pallas_call x2, Pallas kernels, product(): pl.pallas_call(functools.partial(product_kernel, start, block), grid_spec...  24.3 us
    all_to_all x1, starting transfers between devices, on_device(): parts = lax.all_to_all(partial, ('chan', 'blk'), 0, 0, tiled=True)  14.9 us
    pallas_call x3, Pallas kernels, finish(): pl.pallas_call(functools.partial(finish_kernel, start, chunks, adds, writ...  14.8 us
    all_to_all x2, starting transfers between devices, exchange(): return lax.all_to_all(parts, 'chan', 0, 0, tiled=True).reshape(tiles.shape)  9.54 us
    pallas_call x1, Pallas kernels, recouple(): pl.pallas_call(functools.partial(recouple_kernel, sizes), grid_spec=pltpu...  6.56 us
    all_to_all x1, waiting for transfers between devices, on_device(): parts = lax.all_to_all(partial, ('chan', 'blk'), 0, 0, tiled=True)  5.19 us
  transfers between devices with their start and end apart: 3, of which 3 were waited for; matrix products, arithmetic and copies ran while one was open for 0% of the time, Pallas kernels for 14%

profile of v3, /device:TPU:1, one launch (start us, length us, event | category | flops | bytes accessed | tf_op | source)
XLA Modules:
  0.0 177.6 jit_solution(4723847276873498786)
XLA Ops:
  0.6 6.6 %shard_map.77 = (bf16[96,8,3072]{2,1,0:T(8,128)(2,1)}, s32[16,128]{1,0:T(8,128)}, f32[16,128]{1,0:T(8,128)}, s32[8,128]{1,0:T(8,128)}) custom-call(s32[32]{0:T(128)} %live_hbm.1, s32[2,32,384]{2,1,0:T(8,128)} %map_hbm.1, f32[2,32,384]{2,1,0:T(8,128)} %sixj_hbm.1, bf16[96,8,3072]{2,1,0:T(8,128)(2,1)} %bitcast.21), custom_call_target="tpu_custom_call" | custom-call | tf_op jit(solution)/shard_map/pallas_call | solution.py:147
  7.2 63.4 %all_to_all.27 = bf16[16,6,8,3072]{3,2,1,0:T(8,128)(2,1)} all-to-all(bf16[16,6,8,3072]{3,2,1,0:T(8,128)(2,1)} %bitcast.22), channel_id=1, replica_groups=mesh['chan'=16,'blk'=8] {'chan'}, dimensions={0} | all-to-all | bytes 9437184 | tf_op jit(solution)/shard_map/all_to_all | solution.py:378
  70.6 9.3 %shard_map.79 = bf16[96,8,1024]{2,1,0:T(8,128)(2,1)} custom-call(s32[8,128]{1,0:T(8,128)} %get-tuple-element.10.arrival_hbm, bf16[96,8,3072]{2,1,0:T(8,128)(2,1)} %bitcast.13, bf16[2,3072,3072]{2,1,0:T(8,128)(2,1)} %w_ref.3), custom_call_target="tpu_custom_call" | custom-call | flops 4831838208 | bytes 18874368 | tf_op jit(solution)/shard_map/pallas_call | solution.py:252
  79.9 4.6 %all-to-all-start.2 = ((bf16[16,6,8,1024]{3,2,1,0:T(8,128)(2,1)}), bf16[16,6,8,1024]{3,2,1,0:T(8,128)(2,1)}, u32[]{:S(2)}, u32[]{:S(2)}) async-start(bf16[16,6,8,1024]{3,2,1,0:T(8,128)(2,1)} %bitcast.19), calls=%async_computation.2 | async-start | bytes 3145728 | tf_op jit(solution)/shard_map/all_to_all | solution.py:378
  84.6 15.0 %shard_map.78 = bf16[96,8,2048]{2,1,0:T(8,128)(2,1)} custom-call(s32[8,128]{1,0:T(8,128)} %get-tuple-element.10.arrival_hbm, bf16[96,8,3072]{2,1,0:T(8,128)(2,1)} %bitcast.14, bf16[2,3072,3072]{2,1,0:T(8,128)(2,1)} %w_ref.3), custom_call_target="tpu_custom_call" | custom-call | flops 9663676416 | bytes 33030144 | tf_op jit(solution)/shard_map/pallas_call | solution.py:252
  99.6 5.3 %all-to-all-done.2 = bf16[16,6,8,1024]{3,2,1,0:T(8,128)(2,1)} async-done(((bf16[16,6,8,1024]{3,2,1,0:T(8,128)(2,1)}), bf16[16,6,8,1024]{3,2,1,0:T(8,128)(2,1)}, u32[]{:S(2)}, u32[]{:S(2)}) %all-to-all-start.2) | async-done | bytes 1572896 | tf_op jit(solution)/shard_map/all_to_all | solution.py:378
  104.9 4.9 %all-to-all-start.1 = ((bf16[16,6,8,2048]{3,2,1,0:T(8,128)(2,1)}), bf16[16,6,8,2048]{3,2,1,0:T(8,128)(2,1)}, u32[]{:S(2)}, u32[]{:S(2)}) async-start(bf16[16,6,8,2048]{3,2,1,0:T(8,128)(2,1)} %bitcast.18), calls=%async_computation.1 | async-start | bytes 6291456 | tf_op jit(solution)/shard_map/all_to_all | solution.py:378
  109.8 4.9 %shard_map.80 = (bf16[96,8,3072]{2,1,0:T(8,128)(2,1)}, f32[128,128]{1,0:T(8,128)}) custom-call(s32[16,128]{1,0:T(8,128)} %get-tuple-element.8.ints_hbm, f32[16,128]{1,0:T(8,128)} %get-tuple-element.9.coefs_hbm, bf16[96,8,1024]{2,1,0:T(8,128)(2,1)} %bitcast.7.back_ref, bf16[96,8,3072]{2,1,0:T(8,128)(2,1)} %bitcast.15), custom_call_target="tpu_custom_call" | custom-call | flops 4718592 | bytes 4718592 | tf_op jit(solution)/shard_map/pallas_call | solution.py:347
  114.7 30.5 %all-to-all-done.1 = bf16[16,6,8,2048]{3,2,1,0:T(8,128)(2,1)} async-done(((bf16[16,6,8,2048]{3,2,1,0:T(8,128)(2,1)}), bf16[16,6,8,2048]{3,2,1,0:T(8,128)(2,1)}, u32[]{:S(2)}, u32[]{:S(2)}) %all-to-all-start.1) | async-done | bytes 3145760 | tf_op jit(solution)/shard_map/all_to_all | solution.py:378
  145.1 5.7 %shard_map.82 = f32[128,128]{1,0:T(8,128)} custom-call(s32[16,128]{1,0:T(8,128)} %get-tuple-element.8.ints_hbm, f32[16,128]{1,0:T(8,128)} %get-tuple-element.9.coefs_hbm, bf16[96,8,2048]{2,1,0:T(8,128)(2,1)} %bitcast.4.back_ref, bf16[96,8,3072]{2,1,0:T(8,128)(2,1)} %bitcast.16, f32[128,128]{1,0:T(8,128)} %get-tuple-element.13.refs_0_), custom_call_target="tpu_custom_call" | custom-call | flops 9437184 | bytes 9437184 | tf_op jit(solution)/shard_map/pallas_call | solution.py:347
  150.8 14.9 %all-to-all-start.3 = ((f32[128,1,128]{2,1,0:T(1,128)}), f32[128,1,128]{2,1,0:T(1,128)S(1)}, u32[]{:S(2)}, u32[]{:S(2)}) async-start(f32[128,1,128]{2,1,0:T(1,128)} %bitcast.23), calls=%async_computation.3 | async-start | bytes 131072 | tf_op jit(solution)/shard_map/all_to_all | solution.py:407
  165.7 4.3 %shard_map.81 = bf16[96,8,3072]{2,1,0:T(8,128)(2,1)} custom-call(s32[16,128]{1,0:T(8,128)} %get-tuple-element.8.ints_hbm, f32[16,128]{1,0:T(8,128)} %get-tuple-element.9.coefs_hbm, bf16[96,8,2048]{2,1,0:T(8,128)(2,1)} %bitcast.4.back_ref, bf16[96,8,3072]{2,1,0:T(8,128)(2,1)} %bitcast.17, ...), custom_call_target="tpu_custom_call", output_to_operand_aliasing={{}: (4, {})} | custom-call | flops 9437184 | bytes 9437184 | tf_op jit(solution)/shard_map/pallas_call | solution.py:347
  170.0 5.2 %all-to-all-done.3 = f32[128,1,128]{2,1,0:T(1,128)S(1)} async-done(((f32[128,1,128]{2,1,0:T(1,128)}), f32[128,1,128]{2,1,0:T(1,128)S(1)}, u32[]{:S(2)}, u32[]{:S(2)}) %all-to-all-start.3) | async-done | bytes 65568 | tf_op jit(solution)/shard_map/all_to_all | solution.py:407
  175.2 0.6 slice_reduce_fusion
Async XLA Ops:
  79.9 25.0 %all-to-all-start.2 = ((bf16[16,6,8,1024]{3,2,1,0:T(8,128)(2,1)}), bf16[16,6,8,1024]{3,2,1,0:T(8,128)(2,1)}, u32[]{:S(2)}, u32[]{:S(2)}) async-start(bf16[16,6,8,1024]{3,2,1,0:T(8,128)(2,1)} %bitcast.19), calls=%async_computation.2 | async-start | bytes 3145728 | tf_op jit(solution)/shard_map/all_to_all | solution.py:378
  104.9 40.2 %all-to-all-start.1 = ((bf16[16,6,8,2048]{3,2,1,0:T(8,128)(2,1)}), bf16[16,6,8,2048]{3,2,1,0:T(8,128)(2,1)}, u32[]{:S(2)}, u32[]{:S(2)}) async-start(bf16[16,6,8,2048]{3,2,1,0:T(8,128)(2,1)} %bitcast.18), calls=%async_computation.1 | async-start | bytes 6291456 | tf_op jit(solution)/shard_map/all_to_all | solution.py:378
  150.8 24.4 %all-to-all-start.3 = ((f32[128,1,128]{2,1,0:T(1,128)}), f32[128,1,128]{2,1,0:T(1,128)S(1)}, u32[]{:S(2)}, u32[]{:S(2)}) async-start(f32[128,1,128]{2,1,0:T(1,128)} %bitcast.23), calls=%async_computation.3 | async-start | bytes 131072 | tf_op jit(solution)/shard_map/all_to_all | solution.py:407

commit v4 on v3

--- a/solution.py
+++ b/solution.py
@@ -69,6 +69,8 @@
 
     for copy in from_hbm:
         copy.wait()
+    for copy in incoming[1:]:
+        copy.start()
     source = None
     local = []
     for term in range(2):
@@ -102,7 +104,7 @@
         pltpu.make_async_copy(ints_ref, ints, table_sem.at[0]),
         pltpu.make_async_copy(coefs_ref, coefs, table_sem.at[1]),
     ]
-    for copy in to_smem + incoming[1:]:
+    for copy in to_smem:
         copy.start()
 
     row = lax.broadcasted_iota(jnp.int32, (chan_count, LANES), 0)
@@ -115,7 +117,7 @@
     for copy in to_smem:
         copy.wait()
     width = held.shape[2] // chunks
-    tile_row = lax.broadcasted_iota(jnp.int32, (TILE, width), 0)
+    tile_row = lax.broadcasted_iota(jnp.int32, (TILE, LANES), 0)
     for i in range(chunks):
         incoming[i].wait()
         columns = pl.ds(i * width, width)
@@ -129,12 +131,16 @@
                 live = live_ref[d * chans_dev + c] - first_row
                 first = held[entry & LOW, :, columns].astype(jnp.float32)
                 second = held[(entry >> BITS) & LOW, :, columns].astype(jnp.float32)
-                value = coefs[d, 2 * r] * first + coefs[d, 2 * r + 1] * second
-                value = jnp.where(tile_row < live, value, 0.0)
+                keep = tile_row < live
+                scale = [
+                    jnp.tile(jnp.where(keep, coefs[d, 2 * r + term], 0.0), (1, width // LANES))
+                    for term in range(2)
+                ]
+                value = scale[0] * first + scale[1] * second
                 made[d * bucket + r, :, columns] = value.astype(jnp.bfloat16)
             return carry
 
-        lax.fori_loop(0, chan_count, to_one, 0)
+        lax.fori_loop(0, chan_count, to_one, 0, unroll=2)
         outgoing[i].start()
     for copy in outgoing:
         copy.wait()
@@ -280,10 +286,10 @@
     refs = list(refs)
     if start and writes:
         refs.pop(0)
-    before_ref = refs.pop(0) if start and adds else None
+    before_hbm = refs.pop(0) if start and adds else None
     out_ref = refs.pop(0) if writes else None
     energy_ref = refs.pop(0) if adds else None
-    ints_ref, coefs_ref, back, pair, made, slot_of, weight_of, back_sem, pair_sem, out_sem, table_sem = refs
+    ints_ref, coefs_ref, before_ref, back, pair, made, slot_of, weight_of, back_sem, pair_sem, out_sem, table_sem = refs
     slots, _, columns = back.shape
     bucket = slots // ints_ref.shape[0]
     here = pl.ds(start, columns)
@@ -295,6 +301,9 @@
         pltpu.make_async_copy(ints_hbm, ints_ref, table_sem.at[0]),
         pltpu.make_async_copy(coefs_hbm, coefs_ref, table_sem.at[1]),
     ]
+    if start and adds:
+        earlier = pltpu.make_async_copy(before_hbm, before_ref, table_sem.at[2])
+        tables.append(earlier)
     for copies in [tables] + list(zip(*incoming)):
         for copy in copies:
             copy.start()
@@ -334,7 +343,7 @@
     if adds:
         total = jnp.sum(jnp.sum(total, axis=0, keepdims=True), axis=1, keepdims=True)
         total = jnp.broadcast_to(total, energy_ref.shape)
-        energy_ref[...] = total + before_ref[...] if start else total
+        energy_ref[...] = total + before_ref[0:1, :] if start else total
     for copy in outgoing:
         copy.wait()
 
@@ -348,11 +357,12 @@
         functools.partial(finish_kernel, start, chunks, adds, writes),
         grid_spec=pltpu.PrefetchScalarGridSpec(
             num_scalar_prefetch=0,
-            in_specs=[hbm_spec()] * (4 + again) + [energy] * more,
+            in_specs=[hbm_spec()] * (4 + again + more),
             out_specs=[spec for spec, _ in outs],
             scratch_shapes=[
                 pltpu.SMEM(ints.shape, jnp.int32),
                 pltpu.SMEM(coefs.shape, jnp.float32),
+                pltpu.VMEM((TILE, LANES), jnp.float32),
                 pltpu.VMEM(back.shape, back.dtype),
                 pltpu.VMEM(back.shape, back.dtype),
                 pltpu.VMEM(back.shape, back.dtype),
@@ -361,7 +371,7 @@
                 pltpu.SemaphoreType.DMA((chunks,)),
                 pltpu.SemaphoreType.DMA((chunks,)),
                 pltpu.SemaphoreType.DMA((chunks,)),
-                pltpu.SemaphoreType.DMA((2,)),
+                pltpu.SemaphoreType.DMA((3,)),
             ],
         ),
         out_shape=[shape for _, shape in outs],
@@ -395,15 +405,17 @@
         made = product(arrival, got, ph_coupling, start, width)
         back = exchange(made, chan_count)
         chunks = max(1, 4 * width // columns)
+        last = start + width == columns
+        copies = chan_count * blk_count if last else TILE
         call = functools.partial(
-            finish, ints, coefs, back, pair_tiles, start, cycle_pp, partial, chan_count * blk_count, chunks
+            finish, ints, coefs, back, pair_tiles, start, cycle_pp, partial, copies, chunks
         )
         start += width
-        if start < columns:
-            cycle_pp, partial = call()
-        else:
+        if last:
             (partial,) = call(writes=False)
             (cycle_pp,) = call(adds=False)
+        else:
+            cycle_pp, partial = call()
     parts = lax.all_to_all(partial, ("chan", "blk"), 0, 0, tiled=True)
     energy = jnp.sum(parts[:, 0]) / (columns * math.sqrt(chan_count * chans_dev))
     return (cycle_pp.reshape(pp_amps.shape), energy)

time: 178 us -> 177 us (level)
  no operation moved by 1% of the time
where the time goes in v4:
time: 177 us; the launch traced here: 176 us
  blocking collectives  63.4 us (36%)
  Pallas kernels  44.5 us (25%)
  waiting for transfers between devices  41 us (23%)
  starting transfers between devices  24.4 us (14%)
  between operations  2.48 us (1%)
    all_to_all x1, blocking collectives, exchange(): return lax.all_to_all(parts, 'chan', 0, 0, tiled=True).reshape(tiles.shape)  63.4 us
    all_to_all x2, waiting for transfers between devices, exchange(): return lax.all_to_all(parts, 'chan', 0, 0, tiled=True).reshape(tiles.shape)  35.8 us
    pallas_call x2, Pallas kernels, product(): pl.pallas_call(functools.partial(product_kernel, start, block), grid_spec...  24.3 us
    all_to_all x1, starting transfers between devices, on_device(): parts = lax.all_to_all(partial, ('chan', 'blk'), 0, 0, tiled=True)  14.9 us
    pallas_call x3, Pallas kernels, finish(): pl.pallas_call(functools.partial(finish_kernel, start, chunks, adds, writ...  14 us
    all_to_all x2, starting transfers between devices, exchange(): return lax.all_to_all(parts, 'chan', 0, 0, tiled=True).reshape(tiles.shape)  9.54 us
    pallas_call x1, Pallas kernels, recouple(): pl.pallas_call(functools.partial(recouple_kernel, sizes), grid_spec=pltpu...  6.18 us
    all_to_all x1, waiting for transfers between devices, on_device(): parts = lax.all_to_all(partial, ('chan', 'blk'), 0, 0, tiled=True)  5.18 us
  transfers between devices with their start and end apart: 3, of which 3 were waited for; matrix products, arithmetic and copies ran while one was open for 0% of the time, Pallas kernels for 14%

profile of v4, /device:TPU:1, one launch (start us, length us, event | category | flops | bytes accessed | tf_op | source)
XLA Modules:
  0.0 176.4 jit_solution(15672659746229132079)
XLA Ops:
  0.6 6.2 %shard_map.77 = (bf16[96,8,3072]{2,1,0:T(8,128)(2,1)}, s32[16,128]{1,0:T(8,128)}, f32[16,128]{1,0:T(8,128)}, s32[8,128]{1,0:T(8,128)}) custom-call(s32[32]{0:T(128)} %live_hbm.1, s32[2,32,384]{2,1,0:T(8,128)} %map_hbm.1, f32[2,32,384]{2,1,0:T(8,128)} %sixj_hbm.1, bf16[96,8,3072]{2,1,0:T(8,128)(2,1)} %bitcast.21), custom_call_target="tpu_custom_call" | custom-call | tf_op jit(solution)/shard_map/pallas_call | solution.py:153
  6.8 63.4 %all_to_all.27 = bf16[16,6,8,3072]{3,2,1,0:T(8,128)(2,1)} all-to-all(bf16[16,6,8,3072]{3,2,1,0:T(8,128)(2,1)} %bitcast.22), channel_id=1, replica_groups=mesh['chan'=16,'blk'=8] {'chan'}, dimensions={0} | all-to-all | bytes 9437184 | tf_op jit(solution)/shard_map/all_to_all | solution.py:388
  70.2 9.3 %shard_map.79 = bf16[96,8,1024]{2,1,0:T(8,128)(2,1)} custom-call(s32[8,128]{1,0:T(8,128)} %get-tuple-element.10.arrival_hbm, bf16[96,8,3072]{2,1,0:T(8,128)(2,1)} %bitcast.13, bf16[2,3072,3072]{2,1,0:T(8,128)(2,1)} %w_ref.3), custom_call_target="tpu_custom_call" | custom-call | flops 4831838208 | bytes 18874368 | tf_op jit(solution)/shard_map/pallas_call | solution.py:258
  79.5 4.6 %all-to-all-start.2 = ((bf16[16,6,8,1024]{3,2,1,0:T(8,128)(2,1)}), bf16[16,6,8,1024]{3,2,1,0:T(8,128)(2,1)}, u32[]{:S(2)}, u32[]{:S(2)}) async-start(bf16[16,6,8,1024]{3,2,1,0:T(8,128)(2,1)} %bitcast.19), calls=%async_computation.2 | async-start | bytes 3145728 | tf_op jit(solution)/shard_map/all_to_all | solution.py:388
  84.2 15.0 %shard_map.78 = bf16[96,8,2048]{2,1,0:T(8,128)(2,1)} custom-call(s32[8,128]{1,0:T(8,128)} %get-tuple-element.10.arrival_hbm, bf16[96,8,3072]{2,1,0:T(8,128)(2,1)} %bitcast.14, bf16[2,3072,3072]{2,1,0:T(8,128)(2,1)} %w_ref.3), custom_call_target="tpu_custom_call" | custom-call | flops 9663676416 | bytes 33030144 | tf_op jit(solution)/shard_map/pallas_call | solution.py:258
  99.2 5.3 %all-to-all-done.2 = bf16[16,6,8,1024]{3,2,1,0:T(8,128)(2,1)} async-done(((bf16[16,6,8,1024]{3,2,1,0:T(8,128)(2,1)}), bf16[16,6,8,1024]{3,2,1,0:T(8,128)(2,1)}, u32[]{:S(2)}, u32[]{:S(2)}) %all-to-all-start.2) | async-done | bytes 1572896 | tf_op jit(solution)/shard_map/all_to_all | solution.py:388
  104.5 4.9 %all-to-all-start.1 = ((bf16[16,6,8,2048]{3,2,1,0:T(8,128)(2,1)}), bf16[16,6,8,2048]{3,2,1,0:T(8,128)(2,1)}, u32[]{:S(2)}, u32[]{:S(2)}) async-start(bf16[16,6,8,2048]{3,2,1,0:T(8,128)(2,1)} %bitcast.18), calls=%async_computation.1 | async-start | bytes 6291456 | tf_op jit(solution)/shard_map/all_to_all | solution.py:388
  109.4 4.8 %shard_map.80 = (bf16[96,8,3072]{2,1,0:T(8,128)(2,1)}, f32[8,128]{1,0:T(8,128)}) custom-call(s32[16,128]{1,0:T(8,128)} %get-tuple-element.8.ints_hbm, f32[16,128]{1,0:T(8,128)} %get-tuple-element.9.coefs_hbm, bf16[96,8,1024]{2,1,0:T(8,128)(2,1)} %bitcast.7.back_ref, bf16[96,8,3072]{2,1,0:T(8,128)(2,1)} %bitcast.15), custom_call_target="tpu_custom_call" | custom-call | flops 4718592 | bytes 4718592 | tf_op jit(solution)/shard_map/pallas_call | solution.py:356
  114.3 30.5 %all-to-all-done.1 = bf16[16,6,8,2048]{3,2,1,0:T(8,128)(2,1)} async-done(((bf16[16,6,8,2048]{3,2,1,0:T(8,128)(2,1)}), bf16[16,6,8,2048]{3,2,1,0:T(8,128)(2,1)}, u32[]{:S(2)}, u32[]{:S(2)}) %all-to-all-start.1) | async-done | bytes 3145760 | tf_op jit(solution)/shard_map/all_to_all | solution.py:388
  144.8 4.8 %shard_map.82 = f32[128,128]{1,0:T(8,128)} custom-call(s32[16,128]{1,0:T(8,128)} %get-tuple-element.8.ints_hbm, f32[16,128]{1,0:T(8,128)} %get-tuple-element.9.coefs_hbm, bf16[96,8,2048]{2,1,0:T(8,128)(2,1)} %bitcast.4.back_ref, bf16[96,8,3072]{2,1,0:T(8,128)(2,1)} %bitcast.16, f32[8,128]{1,0:T(8,128)} %get-tuple-element.13.refs_0_), custom_call_target="tpu_custom_call" | custom-call | flops 9437184 | bytes 9437184 | tf_op jit(solution)/shard_map/pallas_call | solution.py:356
  149.6 14.9 %all-to-all-start.3 = ((f32[128,1,128]{2,1,0:T(1,128)}), f32[128,1,128]{2,1,0:T(1,128)S(1)}, u32[]{:S(2)}, u32[]{:S(2)}) async-start(f32[128,1,128]{2,1,0:T(1,128)} %bitcast.23), calls=%async_computation.3 | async-start | bytes 131072 | tf_op jit(solution)/shard_map/all_to_all | solution.py:419
  164.5 4.3 %shard_map.81 = bf16[96,8,3072]{2,1,0:T(8,128)(2,1)} custom-call(s32[16,128]{1,0:T(8,128)} %get-tuple-element.8.ints_hbm, f32[16,128]{1,0:T(8,128)} %get-tuple-element.9.coefs_hbm, bf16[96,8,2048]{2,1,0:T(8,128)(2,1)} %bitcast.4.back_ref, bf16[96,8,3072]{2,1,0:T(8,128)(2,1)} %bitcast.17, ...), custom_call_target="tpu_custom_call", output_to_operand_aliasing={{}: (4, {})} | custom-call | flops 9437184 | bytes 9437184 | tf_op jit(solution)/shard_map/pallas_call | solution.py:356
  168.8 5.2 %all-to-all-done.3 = f32[128,1,128]{2,1,0:T(1,128)S(1)} async-done(((f32[128,1,128]{2,1,0:T(1,128)}), f32[128,1,128]{2,1,0:T(1,128)S(1)}, u32[]{:S(2)}, u32[]{:S(2)}) %all-to-all-start.3) | async-done | bytes 65568 | tf_op jit(solution)/shard_map/all_to_all | solution.py:419
  174.0 0.6 slice_reduce_fusion
Async XLA Ops:
  79.5 25.0 %all-to-all-start.2 = ((bf16[16,6,8,1024]{3,2,1,0:T(8,128)(2,1)}), bf16[16,6,8,1024]{3,2,1,0:T(8,128)(2,1)}, u32[]{:S(2)}, u32[]{:S(2)}) async-start(bf16[16,6,8,1024]{3,2,1,0:T(8,128)(2,1)} %bitcast.19), calls=%async_computation.2 | async-start | bytes 3145728 | tf_op jit(solution)/shard_map/all_to_all | solution.py:388
  104.5 40.2 %all-to-all-start.1 = ((bf16[16,6,8,2048]{3,2,1,0:T(8,128)(2,1)}), bf16[16,6,8,2048]{3,2,1,0:T(8,128)(2,1)}, u32[]{:S(2)}, u32[]{:S(2)}) async-start(bf16[16,6,8,2048]{3,2,1,0:T(8,128)(2,1)} %bitcast.18), calls=%async_computation.1 | async-start | bytes 6291456 | tf_op jit(solution)/shard_map/all_to_all | solution.py:388
  149.6 24.4 %all-to-all-start.3 = ((f32[128,1,128]{2,1,0:T(1,128)}), f32[128,1,128]{2,1,0:T(1,128)S(1)}, u32[]{:S(2)}, u32[]{:S(2)}) async-start(f32[128,1,128]{2,1,0:T(1,128)} %bitcast.23), calls=%async_computation.3 | async-start | bytes 131072 | tf_op jit(solution)/shard_map/all_to_all | solution.py:419

commit v5 on v4

--- a/solution.py
+++ b/solution.py
@@ -203,9 +203,13 @@
         at = pl.ds(pl.multiple_of(n * block, block), block)
         return pltpu.make_async_copy(made.at[:, :, at], out_ref.at[:, :, at], out_sem.at[n])
 
-    def each(c, action):
+    def x_all(c):
+        tiles = pl.ds(c * part, part)
+        return pltpu.make_async_copy(x_ref.at[tiles], rows.at[tiles], x_sem.at[c])
+
+    def start_x(c):
         def one(j, carry):
-            action(x_copy(j, c))
+            x_copy(j, c).start()
             return carry
 
         lax.fori_loop(c * part, (c + 1) * part, one, 0, unroll=8)
@@ -217,26 +221,26 @@
     for c in range(chans_dev):
         if c:
             w_copy(0, c).start()
-        each(c, lambda copy: copy.start())
-    for k in range(chans_dev, min(depth, steps * chans_dev)):
-        w_copy(k // chans_dev, k % chans_dev).start()
+        start_x(c)
 
     def step(n, first):
         at = pl.ds(pl.multiple_of(n * block, block), block)
         for c in range(chans_dev):
             if first:
-                each(c, lambda copy: copy.wait())
+                x_all(c).wait()
             w_copy(n, c).wait()
+            later = n * chans_dev + c + 2
+
+            @pl.when(later < steps * chans_dev)
+            def _():
+                w_copy(later // chans_dev, later % chans_dev).start()
+
             left = rows[pl.ds(c * part, part)].reshape(part * TILE, columns)
             slot = lax.rem(n * chans_dev + c, depth)
             result = jnp.dot(left, w_held[slot], preferred_element_type=jnp.float32)
             result = result.astype(jnp.bfloat16).reshape(part, TILE, block)
             for i in range(part):
                 made[arrival_ref[0, c * part + i], :, at] = result[i]
-
-            @pl.when(n + depth // chans_dev < steps)
-            def _():
-                w_copy(n + depth // chans_dev, c).start()
 
         out_copy(n).start()
 

time: 177 us -> 177 us (level)
  no operation moved by 1% of the time
where the time goes in v5:
time: 177 us; the launch traced here: 176 us
  blocking collectives  63.4 us (36%)
  Pallas kernels  44.5 us (25%)
  waiting for transfers between devices  40.9 us (23%)
  starting transfers between devices  24.5 us (14%)
  between operations  2.48 us (1%)
    all_to_all x1, blocking collectives, exchange(): return lax.all_to_all(parts, 'chan', 0, 0, tiled=True).reshape(tiles.shape)  63.4 us
    all_to_all x2, waiting for transfers between devices, exchange(): return lax.all_to_all(parts, 'chan', 0, 0, tiled=True).reshape(tiles.shape)  35.8 us
    pallas_call x2, Pallas kernels, product(): pl.pallas_call(functools.partial(product_kernel, start, block), grid_spec...  24.4 us
    all_to_all x1, starting transfers between devices, on_device(): parts = lax.all_to_all(partial, ('chan', 'blk'), 0, 0, tiled=True)  14.9 us
    pallas_call x3, Pallas kernels, finish(): pl.pallas_call(functools.partial(finish_kernel, start, chunks, adds, writ...  14 us
    all_to_all x2, starting transfers between devices, exchange(): return lax.all_to_all(parts, 'chan', 0, 0, tiled=True).reshape(tiles.shape)  9.55 us
    pallas_call x1, Pallas kernels, recouple(): pl.pallas_call(functools.partial(recouple_kernel, sizes), grid_spec=pltpu...  6.18 us
    all_to_all x1, waiting for transfers between devices, on_device(): parts = lax.all_to_all(partial, ('chan', 'blk'), 0, 0, tiled=True)  5.18 us
  transfers between devices with their start and end apart: 3, of which 3 were waited for; matrix products, arithmetic and copies ran while one was open for 0% of the time, Pallas kernels for 14%

profile of v5, /device:TPU:1, one launch (start us, length us, event | category | flops | bytes accessed | tf_op | source)
XLA Modules:
  0.0 176.4 jit_solution(5246154371269542582)
XLA Ops:
  0.6 6.2 %shard_map.77 = (bf16[96,8,3072]{2,1,0:T(8,128)(2,1)}, s32[16,128]{1,0:T(8,128)}, f32[16,128]{1,0:T(8,128)}, s32[8,128]{1,0:T(8,128)}) custom-call(s32[32]{0:T(128)} %live_hbm.1, s32[2,32,384]{2,1,0:T(8,128)} %map_hbm.1, f32[2,32,384]{2,1,0:T(8,128)} %sixj_hbm.1, bf16[96,8,3072]{2,1,0:T(8,128)(2,1)} %bitcast.21), custom_call_target="tpu_custom_call" | custom-call | tf_op jit(solution)/shard_map/pallas_call | solution.py:153
  6.8 63.4 %all_to_all.27 = bf16[16,6,8,3072]{3,2,1,0:T(8,128)(2,1)} all-to-all(bf16[16,6,8,3072]{3,2,1,0:T(8,128)(2,1)} %bitcast.22), channel_id=1, replica_groups=mesh['chan'=16,'blk'=8] {'chan'}, dimensions={0} | all-to-all | bytes 9437184 | tf_op jit(solution)/shard_map/all_to_all | solution.py:392
  70.2 9.3 %shard_map.79 = bf16[96,8,1024]{2,1,0:T(8,128)(2,1)} custom-call(s32[8,128]{1,0:T(8,128)} %get-tuple-element.10.arrival_hbm, bf16[96,8,3072]{2,1,0:T(8,128)(2,1)} %bitcast.13, bf16[2,3072,3072]{2,1,0:T(8,128)(2,1)} %w_ref.3), custom_call_target="tpu_custom_call" | custom-call | flops 4831838208 | bytes 18874368 | tf_op jit(solution)/shard_map/pallas_call | solution.py:262
  79.5 4.6 %all-to-all-start.2 = ((bf16[16,6,8,1024]{3,2,1,0:T(8,128)(2,1)}), bf16[16,6,8,1024]{3,2,1,0:T(8,128)(2,1)}, u32[]{:S(2)}, u32[]{:S(2)}) async-start(bf16[16,6,8,1024]{3,2,1,0:T(8,128)(2,1)} %bitcast.19), calls=%async_computation.2 | async-start | bytes 3145728 | tf_op jit(solution)/shard_map/all_to_all | solution.py:392
  84.2 15.0 %shard_map.78 = bf16[96,8,2048]{2,1,0:T(8,128)(2,1)} custom-call(s32[8,128]{1,0:T(8,128)} %get-tuple-element.10.arrival_hbm, bf16[96,8,3072]{2,1,0:T(8,128)(2,1)} %bitcast.14, bf16[2,3072,3072]{2,1,0:T(8,128)(2,1)} %w_ref.3), custom_call_target="tpu_custom_call" | custom-call | flops 9663676416 | bytes 33030144 | tf_op jit(solution)/shard_map/pallas_call | solution.py:262
  99.2 5.3 %all-to-all-done.2 = bf16[16,6,8,1024]{3,2,1,0:T(8,128)(2,1)} async-done(((bf16[16,6,8,1024]{3,2,1,0:T(8,128)(2,1)}), bf16[16,6,8,1024]{3,2,1,0:T(8,128)(2,1)}, u32[]{:S(2)}, u32[]{:S(2)}) %all-to-all-start.2) | async-done | bytes 1572896 | tf_op jit(solution)/shard_map/all_to_all | solution.py:392
  104.5 4.9 %all-to-all-start.1 = ((bf16[16,6,8,2048]{3,2,1,0:T(8,128)(2,1)}), bf16[16,6,8,2048]{3,2,1,0:T(8,128)(2,1)}, u32[]{:S(2)}, u32[]{:S(2)}) async-start(bf16[16,6,8,2048]{3,2,1,0:T(8,128)(2,1)} %bitcast.18), calls=%async_computation.1 | async-start | bytes 6291456 | tf_op jit(solution)/shard_map/all_to_all | solution.py:392
  109.4 4.8 %shard_map.80 = (bf16[96,8,3072]{2,1,0:T(8,128)(2,1)}, f32[8,128]{1,0:T(8,128)}) custom-call(s32[16,128]{1,0:T(8,128)} %get-tuple-element.8.ints_hbm, f32[16,128]{1,0:T(8,128)} %get-tuple-element.9.coefs_hbm, bf16[96,8,1024]{2,1,0:T(8,128)(2,1)} %bitcast.7.back_ref, bf16[96,8,3072]{2,1,0:T(8,128)(2,1)} %bitcast.15), custom_call_target="tpu_custom_call" | custom-call | flops 4718592 | bytes 4718592 | tf_op jit(solution)/shard_map/pallas_call | solution.py:360
  114.3 30.5 %all-to-all-done.1 = bf16[16,6,8,2048]{3,2,1,0:T(8,128)(2,1)} async-done(((bf16[16,6,8,2048]{3,2,1,0:T(8,128)(2,1)}), bf16[16,6,8,2048]{3,2,1,0:T(8,128)(2,1)}, u32[]{:S(2)}, u32[]{:S(2)}) %all-to-all-start.1) | async-done | bytes 3145760 | tf_op jit(solution)/shard_map/all_to_all | solution.py:392
  144.8 4.8 %shard_map.82 = f32[128,128]{1,0:T(8,128)} custom-call(s32[16,128]{1,0:T(8,128)} %get-tuple-element.8.ints_hbm, f32[16,128]{1,0:T(8,128)} %get-tuple-element.9.coefs_hbm, bf16[96,8,2048]{2,1,0:T(8,128)(2,1)} %bitcast.4.back_ref, bf16[96,8,3072]{2,1,0:T(8,128)(2,1)} %bitcast.16, f32[8,128]{1,0:T(8,128)} %get-tuple-element.13.refs_0_), custom_call_target="tpu_custom_call" | custom-call | flops 9437184 | bytes 9437184 | tf_op jit(solution)/shard_map/pallas_call | solution.py:360
  149.6 14.9 %all-to-all-start.3 = ((f32[128,1,128]{2,1,0:T(1,128)}), f32[128,1,128]{2,1,0:T(1,128)S(1)}, u32[]{:S(2)}, u32[]{:S(2)}) async-start(f32[128,1,128]{2,1,0:T(1,128)} %bitcast.23), calls=%async_computation.3 | async-start | bytes 131072 | tf_op jit(solution)/shard_map/all_to_all | solution.py:423
  164.5 4.3 %shard_map.81 = bf16[96,8,3072]{2,1,0:T(8,128)(2,1)} custom-call(s32[16,128]{1,0:T(8,128)} %get-tuple-element.8.ints_hbm, f32[16,128]{1,0:T(8,128)} %get-tuple-element.9.coefs_hbm, bf16[96,8,2048]{2,1,0:T(8,128)(2,1)} %bitcast.4.back_ref, bf16[96,8,3072]{2,1,0:T(8,128)(2,1)} %bitcast.17, ...), custom_call_target="tpu_custom_call", output_to_operand_aliasing={{}: (4, {})} | custom-call | flops 9437184 | bytes 9437184 | tf_op jit(solution)/shard_map/pallas_call | solution.py:360
  168.8 5.2 %all-to-all-done.3 = f32[128,1,128]{2,1,0:T(1,128)S(1)} async-done(((f32[128,1,128]{2,1,0:T(1,128)}), f32[128,1,128]{2,1,0:T(1,128)S(1)}, u32[]{:S(2)}, u32[]{:S(2)}) %all-to-all-start.3) | async-done | bytes 65568 | tf_op jit(solution)/shard_map/all_to_all | solution.py:423
  174.0 0.6 slice_reduce_fusion
Async XLA Ops:
  79.5 25.0 %all-to-all-start.2 = ((bf16[16,6,8,1024]{3,2,1,0:T(8,128)(2,1)}), bf16[16,6,8,1024]{3,2,1,0:T(8,128)(2,1)}, u32[]{:S(2)}, u32[]{:S(2)}) async-start(bf16[16,6,8,1024]{3,2,1,0:T(8,128)(2,1)} %bitcast.19), calls=%async_computation.2 | async-start | bytes 3145728 | tf_op jit(solution)/shard_map/all_to_all | solution.py:392
  104.5 40.3 %all-to-all-start.1 = ((bf16[16,6,8,2048]{3,2,1,0:T(8,128)(2,1)}), bf16[16,6,8,2048]{3,2,1,0:T(8,128)(2,1)}, u32[]{:S(2)}, u32[]{:S(2)}) async-start(bf16[16,6,8,2048]{3,2,1,0:T(8,128)(2,1)} %bitcast.18), calls=%async_computation.1 | async-start | bytes 6291456 | tf_op jit(solution)/shard_map/all_to_all | solution.py:392
  149.6 24.4 %all-to-all-start.3 = ((f32[128,1,128]{2,1,0:T(1,128)}), f32[128,1,128]{2,1,0:T(1,128)S(1)}, u32[]{:S(2)}, u32[]{:S(2)}) async-start(f32[128,1,128]{2,1,0:T(1,128)} %bitcast.23), calls=%async_computation.3 | async-start | bytes 131072 | tf_op jit(solution)/shard_map/all_to_all | solution.py:423

commit v6 on v5

--- a/solution.py
+++ b/solution.py
@@ -415,11 +415,7 @@
             finish, ints, coefs, back, pair_tiles, start, cycle_pp, partial, copies, chunks
         )
         start += width
-        if last:
-            (partial,) = call(writes=False)
-            (cycle_pp,) = call(adds=False)
-        else:
-            cycle_pp, partial = call()
+        cycle_pp, partial = call()
     parts = lax.all_to_all(partial, ("chan", "blk"), 0, 0, tiled=True)
     energy = jnp.sum(parts[:, 0]) / (columns * math.sqrt(chan_count * chans_dev))
     return (cycle_pp.reshape(pp_amps.shape), energy)

time: 177 us -> 178 us (level)
  blocking collectives: 63.4 us -> 87.8 us
  starting transfers between devices: 24.5 us -> 9.56 us
  waiting for transfers between devices: 40.9 us -> 35.8 us
  Pallas kernels: 44.5 us -> 41.4 us
    all_to_all x0 -> x1, blocking collectives: none -> 24.4 us  [on_device(): parts = lax.all_to_all(partial, ('chan', 'blk'), 0, 0, tiled=True)]
    all_to_all x1 -> x0, starting transfers between devices: 14.9 us -> none  [on_device(): parts = lax.all_to_all(partial, ('chan', 'blk'), 0, 0, tiled=True)]
    all_to_all x1 -> x0, waiting for transfers between devices: 5.18 us -> none  [on_device(): parts = lax.all_to_all(partial, ('chan', 'blk'), 0, 0, tiled=True)]
    pallas_call x3 -> x2, Pallas kernels: 14 us -> 10.9 us  [finish(): pl.pallas_call(functools.partial(finish_kernel, start, chunks, adds, writ...]
  transfers between devices with their start and end apart: 3 -> 2, of which waited for: 3 -> 2; matrix products, arithmetic and copies ran while one was open for 0% -> 0% of each run, Pallas kernels for 14% -> 11%
where the time goes in v6:
time: 178 us
  blocking collectives  87.8 us (49%)
  Pallas kernels  41.4 us (23%)
  waiting for transfers between devices  35.8 us (20%)
  starting transfers between devices  9.56 us (5%)
  between operations  2.46 us (1%)
    all_to_all x1, blocking collectives, exchange(): return lax.all_to_all(parts, 'chan', 0, 0, tiled=True).reshape(tiles.shape)  63.4 us
    all_to_all x2, waiting for transfers between devices, exchange(): return lax.all_to_all(parts, 'chan', 0, 0, tiled=True).reshape(tiles.shape)  35.8 us
    all_to_all x1, blocking collectives, on_device(): parts = lax.all_to_all(partial, ('chan', 'blk'), 0, 0, tiled=True)  24.4 us
    pallas_call x2, Pallas kernels, product(): pl.pallas_call(functools.partial(product_kernel, start, block), grid_spec...  24.3 us
    pallas_call x2, Pallas kernels, finish(): pl.pallas_call(functools.partial(finish_kernel, start, chunks, adds, writ...  10.9 us
    all_to_all x2, starting transfers between devices, exchange(): return lax.all_to_all(parts, 'chan', 0, 0, tiled=True).reshape(tiles.shape)  9.56 us
    pallas_call x1, Pallas kernels, recouple(): pl.pallas_call(functools.partial(recouple_kernel, sizes), grid_spec=pltpu...  6.17 us
  transfers between devices with their start and end apart: 2, of which 2 were waited for; matrix products, arithmetic and copies ran while one was open for 0% of the time, Pallas kernels for 11%

profile of v6, /device:TPU:1, one launch (start us, length us, event | category | flops | bytes accessed | tf_op | source)
XLA Modules:
  0.0 177.7 jit_solution(181469677125312793)
XLA Ops:
  0.6 6.2 %shard_map.77 = (bf16[96,8,3072]{2,1,0:T(8,128)(2,1)}, s32[16,128]{1,0:T(8,128)}, f32[16,128]{1,0:T(8,128)}, s32[8,128]{1,0:T(8,128)}) custom-call(s32[32]{0:T(128)} %live_hbm.1, s32[2,32,384]{2,1,0:T(8,128)} %map_hbm.1, f32[2,32,384]{2,1,0:T(8,128)} %sixj_hbm.1, bf16[96,8,3072]{2,1,0:T(8,128)(2,1)} %bitcast.19), custom_call_target="tpu_custom_call" | custom-call | tf_op jit(solution)/shard_map/pallas_call | solution.py:153
  6.8 63.4 %all_to_all.27 = bf16[16,6,8,3072]{3,2,1,0:T(8,128)(2,1)} all-to-all(bf16[16,6,8,3072]{3,2,1,0:T(8,128)(2,1)} %bitcast.20), channel_id=1, replica_groups=mesh['chan'=16,'blk'=8] {'chan'}, dimensions={0} | all-to-all | bytes 9437184 | tf_op jit(solution)/shard_map/all_to_all | solution.py:392
  70.2 9.3 %shard_map.79 = bf16[96,8,1024]{2,1,0:T(8,128)(2,1)} custom-call(s32[8,128]{1,0:T(8,128)} %get-tuple-element.12.arrival_hbm, bf16[96,8,3072]{2,1,0:T(8,128)(2,1)} %bitcast.13, bf16[2,3072,3072]{2,1,0:T(8,128)(2,1)} %w_ref.3), custom_call_target="tpu_custom_call" | custom-call | flops 4831838208 | bytes 18874368 | tf_op jit(solution)/shard_map/pallas_call | solution.py:262
  79.5 4.6 %all-to-all-start.2 = ((bf16[16,6,8,1024]{3,2,1,0:T(8,128)(2,1)}), bf16[16,6,8,1024]{3,2,1,0:T(8,128)(2,1)}, u32[]{:S(2)}, u32[]{:S(2)}) async-start(bf16[16,6,8,1024]{3,2,1,0:T(8,128)(2,1)} %bitcast.18), calls=%async_computation.2 | async-start | bytes 3145728 | tf_op jit(solution)/shard_map/all_to_all | solution.py:392
  84.2 15.0 %shard_map.78 = bf16[96,8,2048]{2,1,0:T(8,128)(2,1)} custom-call(s32[8,128]{1,0:T(8,128)} %get-tuple-element.12.arrival_hbm, bf16[96,8,3072]{2,1,0:T(8,128)(2,1)} %bitcast.14, bf16[2,3072,3072]{2,1,0:T(8,128)(2,1)} %w_ref.3), custom_call_target="tpu_custom_call" | custom-call | flops 9663676416 | bytes 33030144 | tf_op jit(solution)/shard_map/pallas_call | solution.py:262
  99.2 5.3 %all-to-all-done.2 = bf16[16,6,8,1024]{3,2,1,0:T(8,128)(2,1)} async-done(((bf16[16,6,8,1024]{3,2,1,0:T(8,128)(2,1)}), bf16[16,6,8,1024]{3,2,1,0:T(8,128)(2,1)}, u32[]{:S(2)}, u32[]{:S(2)}) %all-to-all-start.2) | async-done | bytes 1572896 | tf_op jit(solution)/shard_map/all_to_all | solution.py:392
  104.5 4.9 %all-to-all-start.1 = ((bf16[16,6,8,2048]{3,2,1,0:T(8,128)(2,1)}), bf16[16,6,8,2048]{3,2,1,0:T(8,128)(2,1)}, u32[]{:S(2)}, u32[]{:S(2)}) async-start(bf16[16,6,8,2048]{3,2,1,0:T(8,128)(2,1)} %bitcast.17), calls=%async_computation.1 | async-start | bytes 6291456 | tf_op jit(solution)/shard_map/all_to_all | solution.py:392
  109.4 4.8 %shard_map.80 = (bf16[96,8,3072]{2,1,0:T(8,128)(2,1)}, f32[8,128]{1,0:T(8,128)}) custom-call(s32[16,128]{1,0:T(8,128)} %get-tuple-element.10.ints_hbm, f32[16,128]{1,0:T(8,128)} %get-tuple-element.11.coefs_hbm, bf16[96,8,1024]{2,1,0:T(8,128)(2,1)} %bitcast.7.back_ref, bf16[96,8,3072]{2,1,0:T(8,128)(2,1)} %bitcast.15), custom_call_target="tpu_custom_call" | custom-call | flops 4718592 | bytes 4718592 | tf_op jit(solution)/shard_map/pallas_call | solution.py:360
  114.3 30.5 %all-to-all-done.1 = bf16[16,6,8,2048]{3,2,1,0:T(8,128)(2,1)} async-done(((bf16[16,6,8,2048]{3,2,1,0:T(8,128)(2,1)}), bf16[16,6,8,2048]{3,2,1,0:T(8,128)(2,1)}, u32[]{:S(2)}, u32[]{:S(2)}) %all-to-all-start.1) | async-done | bytes 3145760 | tf_op jit(solution)/shard_map/all_to_all | solution.py:392
  144.8 6.1 %shard_map.81 = (bf16[96,8,3072]{2,1,0:T(8,128)(2,1)}, f32[128,128]{1,0:T(8,128)}) custom-call(s32[16,128]{1,0:T(8,128)} %get-tuple-element.10.ints_hbm, f32[16,128]{1,0:T(8,128)} %get-tuple-element.11.coefs_hbm, bf16[96,8,2048]{2,1,0:T(8,128)(2,1)} %bitcast.4.back_ref, bf16[96,8,3072]{2,1,0:T(8,128)(2,1)} %bitcast.16, ...), custom_call_target="tpu_custom_call", output_to_operand_aliasing={{0}: (4, {})} | custom-call | flops 9437184 | bytes 9437184 | tf_op jit(solution)/shard_map/pallas_call | solution.py:360
  150.9 24.4 %all_to_all.28 = f32[128,1,128]{2,1,0:T(1,128)S(1)} all-to-all(f32[128,1,128]{2,1,0:T(1,128)} %bitcast.23), channel_id=1, replica_groups=mesh['chan'=16,'blk'=8] {'chan','blk'}, dimensions={0} | all-to-all | bytes 131072 | tf_op jit(solution)/shard_map/all_to_all | solution.py:419
  175.3 0.6 slice_reduce_fusion
Async XLA Ops:
  79.5 25.0 %all-to-all-start.2 = ((bf16[16,6,8,1024]{3,2,1,0:T(8,128)(2,1)}), bf16[16,6,8,1024]{3,2,1,0:T(8,128)(2,1)}, u32[]{:S(2)}, u32[]{:S(2)}) async-start(bf16[16,6,8,1024]{3,2,1,0:T(8,128)(2,1)} %bitcast.18), calls=%async_computation.2 | async-start | bytes 3145728 | tf_op jit(solution)/shard_map/all_to_all | solution.py:392
  104.5 40.3 %all-to-all-start.1 = ((bf16[16,6,8,2048]{3,2,1,0:T(8,128)(2,1)}), bf16[16,6,8,2048]{3,2,1,0:T(8,128)(2,1)}, u32[]{:S(2)}, u32[]{:S(2)}) async-start(bf16[16,6,8,2048]{3,2,1,0:T(8,128)(2,1)} %bitcast.17), calls=%async_computation.1 | async-start | bytes 6291456 | tf_op jit(solution)/shard_map/all_to_all | solution.py:392
